TPU v7x, 128 devices: a whole 4x4x4 slice. The times are simulated.
128 devices in a mesh: ctx: 16 (over y, z_lo, core), mp: 8 (over x, z_hi).
Axes of the slice: x: 4, y: 4, z: 4 (z_hi: 2, z_lo: 2; z = z_hi * 2 + z_lo), core: 2. Of those that a mesh axis runs over, the one named last changes fastest.
Arguments:
- tokens: bfloat16 [8192, 2048], P('ctx'), may hold values from -6 to 6
- cotangent: bfloat16 [8192, 2048], P('ctx'), may hold values from -6 to 6
- gain_attn: float32 [2048], replicated, may hold values from 0.5 to 1.5
- w_query: bfloat16 [2048, 2048], P(None, 'mp'), may hold values from -0.125 to 0.125
- w_key: bfloat16 [2048, 2048], P(None, 'mp'), may hold values from -0.125 to 0.125
- w_value: bfloat16 [2048, 2048], P(None, 'mp'), may hold values from -0.125 to 0.125
- w_out: bfloat16 [2048, 2048], P('mp'), may hold values from -0.5 to 0.5
- gain_moe: float32 [2048], replicated, may hold values from 0.5 to 1.5
- w_router: bfloat16 [2048, 64], replicated, may hold values from -0.0625 to 0.0625
- shared_gate: bfloat16 [2048, 2816], P(None, 'mp'), may hold values from -0.125 to 0.125
- shared_up: bfloat16 [2048, 2816], P(None, 'mp'), may hold values from -0.125 to 0.125
- shared_down: bfloat16 [2816, 2048], P('mp'), may hold values from -0.109375 to 0.109375
- expert_gate: bfloat16 [3, 2048, 1408], P(None, None, 'mp'), may hold values from -0.125 to 0.125
- expert_up: bfloat16 [3, 2048, 1408], P(None, None, 'mp'), may hold values from -0.125 to 0.125
- expert_down: bfloat16 [3, 1408, 2048], P(None, 'mp'), may hold values from -6 to 6
- expert_ids: int32 [8192, 6], P('ctx'), may hold values from 0 to 63, as said below
- pair_order: int32 [16], replicated, may hold values from 0 to 15, each once
Outputs:
- output: bfloat16 [8192, 2048], P('ctx')
- grad_tokens: bfloat16 [8192, 2048], P('ctx')
- grad_gain_attn: float32 [2048], replicated
- grad_w_query: float32 [2048, 2048], P(None, 'mp')
- grad_w_key: float32 [2048, 2048], P(None, 'mp')
- grad_w_value: float32 [2048, 2048], P(None, 'mp')
- grad_w_out: float32 [2048, 2048], P('mp')
- grad_gain_moe: float32 [2048], replicated
- grad_w_router: float32 [2048, 64], replicated
- grad_shared_gate: float32 [2048, 2816], P(None, 'mp')
- grad_shared_up: float32 [2048, 2816], P(None, 'mp')
- grad_shared_down: float32 [2816, 2048], P('mp')
- grad_expert_gate: float32 [3, 2048, 1408], P(None, None, 'mp')
- grad_expert_up: float32 [3, 2048, 1408], P(None, None, 'mp')
- grad_expert_down: float32 [3, 1408, 2048], P(None, 'mp')
Inputs may be any that keep to these rules, and one draw needn't show every extreme that they name: `expert_ids`: each row names 6 different experts. In the rows of one device (aligned blocks of 512 rows) each expert below 3 is named by at most 32 rows, and in every block one of them by exactly 32. A permutation: ctx device i holds blocks pair_order[i] and 31 - pair_order[i] of the sequence.
All inputs are finite; a program needn't handle non-finite values.
Results may differ from a plain program's by a relative error of at most 0.028.
Values may be sent and summed in bfloat16 or wider, within the bound.
A program may use at most 320 MiB of HBM per device.

v0:
```python
import jax
import jax.numpy as jnp
from jax import lax
from jax.sharding import PartitionSpec as P

HD = 128
CAP = 32


EPSILON = 1e-06
ROPE_BASE = 10000.0
PRECISE = lax.Precision.HIGHEST


def matmul(left, right):
    return jnp.dot(left, right, preferred_element_type=jnp.float32)


def contract(pattern, left, right):
    return jnp.einsum(pattern, left, right, preferred_element_type=jnp.float32)


def exact_contract(pattern, left, right):
    return jnp.einsum(pattern, left, right, precision=PRECISE, preferred_element_type=jnp.float32)


def rms_norm(values, gain_vec):
    return (
        values * lax.rsqrt(jnp.mean(values * values, axis=-1, keepdims=True) + EPSILON) * gain_vec
    )


def swiglu(gate_vals, up_vals):
    return jax.nn.silu(gate_vals) * up_vals


def rotate(values, angle_cos, angle_sin):
    half_dim = values.shape[-1] // 2
    first_half = values[..., :half_dim]
    second_half = values[..., half_dim:]
    return jnp.concatenate(
        [
            first_half * angle_cos - second_half * angle_sin,
            second_half * angle_cos + first_half * angle_sin,
        ],
        axis=-1,
    )


def angles(position, head_dim):
    index_range = jnp.arange(head_dim // 2, dtype=jnp.float32)
    inverse = ROPE_BASE ** (-2.0 * index_range / head_dim)
    phase = position.astype(jnp.float32)[:, None] * inverse[None, :]
    return (jnp.cos(phase)[:, None, :], jnp.sin(phase)[:, None, :])


def positions(pair_order, row_count):
    pair_count = pair_order.shape[0]
    half_rows = row_count // 2
    within = jnp.arange(row_count, dtype=jnp.int32)
    first_block = pair_order[:, None] * half_rows + within[None, :]
    second_block = (
        (2 * pair_count - 1 - pair_order[:, None]) * half_rows + within[None, :] - half_rows
    )
    return jnp.where(within[None, :] < half_rows, first_block, second_block).reshape(-1)


def dispatch_table(expert_ids, held_count, slot_count):
    chosen = jnp.any(
        expert_ids[:, :, None] == jnp.arange(held_count, dtype=jnp.int32)[None, None, :], axis=1
    )
    held_flag = chosen.astype(jnp.int32)
    slot_index = jnp.cumsum(held_flag, axis=0) - 1
    placed = chosen[:, :, None] & (
        slot_index[:, :, None] == jnp.arange(slot_count, dtype=jnp.int32)[None, None, :]
    )
    return placed.astype(jnp.float32)


def score_block(queries, query_pos, key_rows, key_pos):
    scores = contract("qhd,khd->hqk", queries, key_rows)
    visible = key_pos[None, None, :] <= query_pos[None, :, None]
    return jnp.where(visible, scores, -1e30)


def attend_forward(queries, query_pos, key_rows, value_rows, key_pos):
    scores = score_block(queries, query_pos, key_rows, key_pos)
    row_max = jnp.max(scores, axis=-1, keepdims=True)
    log_total = row_max + jnp.log(jnp.sum(jnp.exp(scores - row_max), axis=-1, keepdims=True))
    weights = jnp.exp(scores - log_total).astype(jnp.bfloat16)
    return (contract("hqk,khd->qhd", weights, value_rows), log_total)


def attend_backward(queries, query_pos, key_rows, value_rows, key_pos, grad_attended, log_total):
    probs_full = jnp.exp(score_block(queries, query_pos, key_rows, key_pos) - log_total)
    grad_weights = contract("qhd,khd->hqk", grad_attended, value_rows)
    row_delta = jnp.sum(probs_full * grad_weights, axis=-1, keepdims=True)
    grad_scores = (probs_full * (grad_weights - row_delta)).astype(jnp.bfloat16)
    grad_queries = contract("hqk,khd->qhd", grad_scores, key_rows)
    grad_keys = contract("hqk,qhd->khd", grad_scores, queries)
    grad_values = contract("hqk,qhd->khd", probs_full.astype(jnp.bfloat16), grad_attended)
    return (grad_queries, grad_keys, grad_values)


def router_backward(router_probs, grad_held, moe_rows_low, w_router):
    held_count = grad_held.shape[1]
    grad_probs = jnp.pad(grad_held, ((0, 0), (0, router_probs.shape[1] - held_count)))
    grad_logits = router_probs * (
        grad_probs - jnp.sum(grad_probs * router_probs, axis=-1, keepdims=True)
    )
    logits_low = grad_logits.astype(jnp.bfloat16)
    return (
        contract("td,te->de", moe_rows_low, logits_low),
        contract("te,de->td", logits_low, w_router),
    )


def on_device(
    tokens,
    cotangent,
    gain_attn,
    w_query,
    w_key,
    w_value,
    w_out,
    gain_moe,
    w_router,
    shared_gate,
    shared_up,
    shared_down,
    expert_gate,
    expert_up,
    expert_down,
    expert_ids,
    pair_order,
):
    row_count = tokens.shape[0]
    head_dim = HD
    local_heads = w_query.shape[1] // head_dim
    head_shape = (row_count, local_heads, head_dim)
    member = lax.axis_index("ctx")
    every_pos = positions(pair_order, row_count)
    my_pos = lax.dynamic_slice_in_dim(every_pos, member * row_count, row_count)
    cos_mine, sin_mine = angles(my_pos, head_dim)
    scale = head_dim ** (-0.5)
    source = tokens.astype(jnp.float32)
    grad_out = cotangent.astype(jnp.float32)
    normed, first_pull = jax.vjp(rms_norm, source, gain_attn)
    normed_low = normed.astype(jnp.bfloat16)
    q_lin = matmul(normed_low, w_query).reshape(head_shape)
    k_lin = matmul(normed_low, w_key).reshape(head_shape)
    v_low = matmul(normed_low, w_value).astype(jnp.bfloat16)
    q_rot = (rotate(q_lin, cos_mine, sin_mine) * scale).astype(jnp.bfloat16)
    k_rot = rotate(k_lin, cos_mine, sin_mine).astype(jnp.bfloat16)
    k_every, v_every = (
        lax.all_gather(k_rot.reshape(row_count, -1), "ctx", axis=0, tiled=True),
        lax.all_gather(v_low, "ctx", axis=0, tiled=True),
    )
    k_every = k_every.reshape(-1, local_heads, head_dim)
    v_every = v_every.reshape(-1, local_heads, head_dim)
    attended, log_total = attend_forward(q_rot, my_pos, k_every, v_every, every_pos)
    attended_low = attended.reshape(row_count, -1).astype(jnp.bfloat16)
    mixed = source + lax.psum(matmul(attended_low, w_out).astype(jnp.bfloat16), "mp").astype(
        jnp.float32
    )
    normed_moe, second_pull = jax.vjp(rms_norm, mixed, gain_moe)
    moe_low = normed_moe.astype(jnp.bfloat16)
    router_probs = jax.nn.softmax(matmul(moe_low, w_router), axis=-1)
    shared_g = matmul(moe_low, shared_gate)
    shared_u = matmul(moe_low, shared_up)
    shared_act, shared_pull = jax.vjp(swiglu, shared_g, shared_u)
    shared_hidden = shared_act.astype(jnp.bfloat16)
    held_count = expert_gate.shape[0]
    slot_table = dispatch_table(expert_ids, held_count, CAP)
    table_low = slot_table.astype(jnp.bfloat16)
    expert_in = contract("tec,td->ecd", table_low, moe_low).astype(jnp.bfloat16)
    gate_slot = exact_contract("tec,te->ec", slot_table, router_probs[:, :held_count])
    expert_g = contract("ecd,edf->ecf", expert_in, expert_gate)
    expert_u = contract("ecd,edf->ecf", expert_in, expert_up)
    expert_act, expert_pull = jax.vjp(swiglu, expert_g, expert_u)
    expert_hidden = expert_act.astype(jnp.bfloat16)
    expert_part = contract("ecf,efd->ecd", expert_hidden, expert_down)
    gated_part = gate_slot[:, :, None] * expert_part
    moe_part = matmul(shared_hidden, shared_down) + exact_contract(
        "tec,ecd->td", slot_table, gated_part
    )
    output_low = (mixed + lax.psum(moe_part.astype(jnp.bfloat16), "mp").astype(jnp.float32)).astype(
        jnp.bfloat16
    )
    grad_shared_down = contract("tf,td->fd", shared_hidden, cotangent)
    grad_shared_hidden = contract("td,fd->tf", cotangent, shared_down)
    g_shared_g, g_shared_u = shared_pull(grad_shared_hidden)
    g_sg = g_shared_g.astype(jnp.bfloat16)
    g_su = g_shared_u.astype(jnp.bfloat16)
    grad_shared_gate = contract("td,tf->df", moe_low, g_sg)
    grad_shared_up = contract("td,tf->df", moe_low, g_su)
    grad_moe_in = contract("tf,df->td", g_sg, shared_gate) + contract("tf,df->td", g_su, shared_up)
    grad_slot = contract("tec,td->ecd", table_low, cotangent)
    grad_expert_out = (gate_slot[:, :, None] * grad_slot).astype(jnp.bfloat16)
    gate_grad_part = jnp.sum(grad_slot * expert_part, axis=-1)
    grad_expert_down = contract("ecf,ecd->efd", expert_hidden, grad_expert_out)
    grad_expert_hidden = contract("ecd,efd->ecf", grad_expert_out, expert_down)
    g_expert_g, g_expert_u = expert_pull(grad_expert_hidden)
    g_eg = g_expert_g.astype(jnp.bfloat16)
    g_eu = g_expert_u.astype(jnp.bfloat16)
    grad_expert_gate = contract("ecd,ecf->edf", expert_in, g_eg)
    grad_expert_up = contract("ecd,ecf->edf", expert_in, g_eu)
    grad_expert_in = contract("ecf,edf->ecd", g_eg, expert_gate) + contract(
        "ecf,edf->ecd", g_eu, expert_up
    )
    grad_moe_in = grad_moe_in + exact_contract("tec,ecd->td", slot_table, grad_expert_in)
    grad_moe_in, gate_grad = (
        lax.psum(grad_moe_in.astype(jnp.bfloat16), "mp").astype(jnp.float32),
        lax.psum(gate_grad_part.astype(jnp.bfloat16), "mp").astype(jnp.float32),
    )
    grad_held = exact_contract("tec,ec->te", slot_table, gate_grad)
    grad_w_router, router_term = router_backward(router_probs, grad_held, moe_low, w_router)
    grad_mixed_norm, grad_gain_moe = second_pull(grad_moe_in + router_term)
    grad_mixed = grad_out + grad_mixed_norm
    grad_attn_low = grad_mixed.astype(jnp.bfloat16)
    grad_w_out = contract("tk,td->kd", attended_low, grad_attn_low)
    grad_attended = (
        contract("td,kd->tk", grad_attn_low, w_out).astype(jnp.bfloat16).reshape(head_shape)
    )
    grad_q, key_part, value_part = attend_backward(
        q_rot, my_pos, k_every, v_every, every_pos, grad_attended, log_total
    )
    grad_k, grad_v = (
        lax.psum_scatter(
            key_part.reshape(k_every.shape[0], -1).astype(jnp.bfloat16),
            "ctx",
            scatter_dimension=0,
            tiled=True,
        ).astype(jnp.float32),
        lax.psum_scatter(
            value_part.reshape(v_every.shape[0], -1).astype(jnp.bfloat16),
            "ctx",
            scatter_dimension=0,
            tiled=True,
        ).astype(jnp.float32),
    )
    grad_q_lin = (
        rotate(grad_q * scale, cos_mine, -sin_mine).reshape(row_count, -1).astype(jnp.bfloat16)
    )
    grad_k_lin = (
        rotate(grad_k.reshape(head_shape), cos_mine, -sin_mine)
        .reshape(row_count, -1)
        .astype(jnp.bfloat16)
    )
    grad_v_lin = grad_v.astype(jnp.bfloat16)
    grad_w_query = contract("td,tk->dk", normed_low, grad_q_lin)
    grad_w_key = contract("td,tk->dk", normed_low, grad_k_lin)
    grad_w_value = contract("td,tk->dk", normed_low, grad_v_lin)
    grad_normed = (
        contract("tk,dk->td", grad_q_lin, w_query)
        + contract("tk,dk->td", grad_k_lin, w_key)
        + contract("tk,dk->td", grad_v_lin, w_value)
    )
    grad_normed = lax.psum(grad_normed.astype(jnp.bfloat16), "mp").astype(jnp.float32)
    grad_source, grad_gain_attn = first_pull(grad_normed)
    grad_tokens = (grad_mixed + grad_source).astype(jnp.bfloat16)
    (
        grad_gain_attn,
        grad_w_query,
        grad_w_key,
        grad_w_value,
        grad_w_out,
        grad_gain_moe,
        grad_w_router,
        grad_shared_gate,
        grad_shared_up,
        grad_shared_down,
        grad_expert_gate,
        grad_expert_up,
        grad_expert_down,
    ) = (
        lax.psum(grad_gain_attn.astype(jnp.bfloat16), "ctx").astype(jnp.float32),
        lax.psum(grad_w_query.astype(jnp.bfloat16), "ctx").astype(jnp.float32),
        lax.psum(grad_w_key.astype(jnp.bfloat16), "ctx").astype(jnp.float32),
        lax.psum(grad_w_value.astype(jnp.bfloat16), "ctx").astype(jnp.float32),
        lax.psum(grad_w_out.astype(jnp.bfloat16), "ctx").astype(jnp.float32),
        lax.psum(grad_gain_moe.astype(jnp.bfloat16), "ctx").astype(jnp.float32),
        lax.psum(grad_w_router.astype(jnp.bfloat16), "ctx").astype(jnp.float32),
        lax.psum(grad_shared_gate.astype(jnp.bfloat16), "ctx").astype(jnp.float32),
        lax.psum(grad_shared_up.astype(jnp.bfloat16), "ctx").astype(jnp.float32),
        lax.psum(grad_shared_down.astype(jnp.bfloat16), "ctx").astype(jnp.float32),
        lax.psum(grad_expert_gate.astype(jnp.bfloat16), "ctx").astype(jnp.float32),
        lax.psum(grad_expert_up.astype(jnp.bfloat16), "ctx").astype(jnp.float32),
        lax.psum(grad_expert_down.astype(jnp.bfloat16), "ctx").astype(jnp.float32),
    )
    return (
        output_low,
        grad_tokens,
        grad_gain_attn,
        grad_w_query,
        grad_w_key,
        grad_w_value,
        grad_w_out,
        grad_gain_moe,
        grad_w_router,
        grad_shared_gate,
        grad_shared_up,
        grad_shared_down,
        grad_expert_gate,
        grad_expert_up,
        grad_expert_down,
    )


def solution(mesh):
    in_specs = (
        P("ctx", None),
        P("ctx", None),
        P(),
        P(None, "mp"),
        P(None, "mp"),
        P(None, "mp"),
        P("mp", None),
        P(),
        P(),
        P(None, "mp"),
        P(None, "mp"),
        P("mp", None),
        P(None, None, "mp"),
        P(None, None, "mp"),
        P(None, "mp", None),
        P("ctx", None),
        P(),
    )
    out_specs = (
        P("ctx", None),
        P("ctx", None),
        P(),
        P(None, "mp"),
        P(None, "mp"),
        P(None, "mp"),
        P("mp", None),
        P(),
        P(),
        P(None, "mp"),
        P(None, "mp"),
        P("mp", None),
        P(None, None, "mp"),
        P(None, None, "mp"),
        P(None, "mp", None),
    )
    return jax.shard_map(
        on_device, mesh=mesh, in_specs=in_specs, out_specs=out_specs, check_vma=False
    )
```

profile of v0, /device:TPU:1, one launch (start us, length us, event | category | flops | bytes accessed | tf_op | source)
XLA Modules:
  0.0 1177.9 jit_solution(419672367689179151)
XLA Ops:
  8.2 2.1 fusion.8
  10.8 2.8 fusion.82
  15.7 2.8 fusion.84
  26.0 3.3 convolution_convert_fusion.16
  29.9 4.6 broadcast_compare_fusion
  34.5 32.6 %all-gather.5.cloned.1.call-done = bf16[8192,256]{0,1:T(8,128)(2,1)} async-done(((bf16[512,256]{0,1:T(8,128)(2,1)}), bf16[8192,256]{0,1:T(8,128)(2,1)}) %all-gather.5.cloned.1.call-update) | async-done | bytes 4194320 | tf_op jit(solution)/shard_map/all_gather | solution.py:156
  67.1 17.3 %select_reduce_fusion = (f32[2,512]{1,0:T(2,128)S(1)}, f32[2,512,8192]{2,1,0:T(8,128)}) fusion(pred[512,8192]{1,0:T(8,128)(4,1)} %broadcast_compare_fusion, bf16[512,2,128]{2,0,1:T(8,128)(2,1)S(1)} %fusion.33, bf16[8192,2,128]{0,2,1:T(8,128)(2,1)} %bitcast.141), kind=kOutput, calls=%fused_computation.4 | convolution fusion | flops 2164259840 | bytes 42209280 | tf_op jit(solution)/shard_map/qhd,khd->hqk/dot_general | solution.py:20
  84.4 15.7 %exponential_reduce_fusion = f32[2,512]{1,0:T(2,128)S(1)} fusion(f32[2,512,8192]{2,1,0:T(8,128)} %get-tuple-element.69, f32[2,512]{1,0:T(2,128)S(1)} %get-tuple-element.68, pred[512,8192]{1,0:T(8,128)(4,1)} %broadcast_compare_fusion), kind=kLoop, calls=%fused_computation.3 | loop fusion | flops 25164800 | bytes 37756928 | tf_op jit(solution)/shard_map/reduce_sum | solution.py:89
  100.1 6.7 all-gather.3.cloned.1.call-done
  106.8 16.6 %fusion.22 = bf16[2,128,512]{2,1,0:T(8,128)(2,1)S(1)} fusion(f32[2,512,8192]{2,1,0:T(8,128)} %get-tuple-element.69, f32[2,512]{1,0:T(2,128)S(1)} %log_add_fusion, pred[512,8192]{1,0:T(8,128)(4,1)} %broadcast_compare_fusion, bf16[8192,256]{1,0:T(8,128)(2,1)} %all-gather.3.cloned.1.call-done), kind=kOutput, calls=%fused_computation.65 | convolution fusion | flops 2172780544 | bytes 42209280 | tf_op jit(solution)/shard_map/hqk,khd->qhd/dot_general | solution.py:20
  124.1 2.1 convolution_convert_fusion.5
  128.3 107.1 %all-reduce.9.cloned.1.call-done = bf16[512,2048]{1,0:T(8,128)(2,1)} async-done(((bf16[512,2048]{1,0:T(8,128)(2,1)}), bf16[512,2048]{1,0:T(8,128)(2,1)}) %all-reduce.9.cloned.1.call-update) | async-done | bytes 2097168 | tf_op jit(solution)/shard_map/psum | solution.py:163
  235.4 3.1 multiply_reduce_fusion.3
  244.3 18.3 %psum.129 = bf16[3,32]{1,0:T(4,128)(2,1)S(1)} all-reduce(bf16[3,32]{1,0:T(4,128)(2,1)S(1)} %get-tuple-element.72), channel_id=1, replica_groups=mesh['ctx'=16,'mp'=8] {'mp'}, use_global_device_ids=true, to_apply=%region_13.14 | all-reduce | flops 96 | bytes 384 | tf_op jit(solution)/shard_map/psum | solution.py:214
  262.7 2.5 fusion.92
  276.8 2.6 fusion.14
  279.7 111.6 %all-reduce.11.cloned.1.call-done = bf16[512,2048]{1,0:T(8,128)(2,1)} async-done(((bf16[512,2048]{1,0:T(8,128)(2,1)}), bf16[512,2048]{1,0:T(8,128)(2,1)}) %all-reduce.11.cloned.1.call-update) | async-done | bytes 2097168 | tf_op jit(solution)/shard_map/psum | solution.py:213
  391.4 4.3 multiply_reduce_fusion.1
  400.6 30.6 %multiply_reduce_fusion = (f32[2,512]{1,0:T(2,128)S(1)}, f32[2,512,8192]{2,1,0:T(8,128)}) fusion(f32[2,512,8192]{2,1,0:T(8,128)} %get-tuple-element.69, f32[2,512]{1,0:T(2,128)S(1)} %log_add_fusion, pred[512,8192]{1,0:T(8,128)(4,1)} %broadcast_compare_fusion, bf16[512,2,128]{0,2,1:T(8,128)(2,1)} %bitcast.150, bf16[8192,256]{1,0:T(8,128)(2,1)} %all-gather.3.cloned.1.call-done), kind=kOutput, calls=%fused_computation.1 | convolution fusion | flops 2181037056 | bytes 75767808 | tf_op jit(solution)/shard_map/qhd,khd->hqk/dot_general | solution.py:20
  431.2 29.1 %multiply_convert_fusion = bf16[2,512,8192]{2,1,0:T(8,128)(2,1)} fusion(f32[2,512,8192]{2,1,0:T(8,128)} %get-tuple-element.78, f32[2,512,8192]{2,1,0:T(8,128)} %get-tuple-element.69, f32[2,512]{1,0:T(2,128)S(1)} %get-tuple-element.77, f32[2,512]{1,0:T(2,128)S(1)} %log_add_fusion, pred[512,8192]{1,0:T(8,128)(4,1)} %broadcast_compare_fusion), kind=kLoop, calls=%fused_computation | loop fusion | flops 41943040 | bytes 88088576 | tf_op jit(solution)/shard_map/convert_element_type | solution.py:98
  460.2 10.3 convolution_convert_fusion.1
  470.6 18.0 %convolution_convert_fusion = bf16[2,128,8192]{2,1,0:T(8,128)(2,1)} fusion(bf16[512,2,128]{0,2,1:T(8,128)(2,1)} %bitcast.151, f32[2,512,8192]{2,1,0:T(8,128)} %get-tuple-element.69, f32[2,512]{1,0:T(2,128)S(1)} %log_add_fusion, pred[512,8192]{1,0:T(8,128)(4,1)} %broadcast_compare_fusion), kind=kOutput, calls=%fused_computation.6 | convolution fusion | flops 2174746624 | bytes 42209280 | tf_op jit(solution)/shard_map/hqk,qhd->khd/dot_general | solution.py:20
  489.3 3.2 fusion.27
  492.6 2.7 fusion.15
  495.3 9.1 fusion.21
  504.4 33.2 %reduce-scatter.3.cloned.1.call-done = bf16[512,256]{0,1:T(8,128)(2,1)} async-done(((bf16[8192,256]{0,1:T(8,128)(2,1)}), bf16[512,256]{0,1:T(8,128)(2,1)}) %reduce-scatter.3.cloned.1.call-update) | async-done | bytes 262160 | tf_op jit(solution)/shard_map/reduce_scatter | solution.py:229
  549.9 4.2 fusion.99
  554.2 2.8 fusion.100
  557.0 48.8 %reduce-scatter.5.cloned.1.call-done = bf16[512,256]{0,1:T(8,128)(2,1)} async-done(((bf16[8192,256]{0,1:T(8,128)(2,1)}), bf16[512,256]{0,1:T(8,128)(2,1)}) %reduce-scatter.5.cloned.1.call-update) | async-done | bytes 262160 | tf_op jit(solution)/shard_map/reduce_scatter | solution.py:235
  605.7 5.9 add_convert_fusion
  612.1 2.8 convolution_convert_fusion.14
  614.9 2.1 convolution_convert_fusion.4
  617.0 2.9 convolution_convert_fusion.3
  619.9 2.1 convolution_convert_fusion.2
  622.1 2.0 convolution_convert_fusion.7
  624.1 2.0 convolution_convert_fusion.6
  626.1 2.1 convolution_convert_fusion.8
  634.5 2.0 convolution_convert_fusion.10
  636.6 163.7 %all-reduce.15.cloned.1.call-done = (bf16[512,2048]{1,0:T(8,128)(2,1)}, bf16[512,2048]{1,0:T(8,128)(2,1)}) async-done(((bf16[512,2048]{1,0:T(8,128)(2,1)}, bf16[512,2048]{1,0:T(8,128)(2,1)}), (bf16[512,2048]{1,0:T(8,128)(2,1)}, bf16[512,2048]{1,0:T(8,128)(2,1)})) %all-reduce.15.cloned.1.call-update) | async-done | bytes 4194320 | tf_op jit(solution)/shard_map/psum | solution.py:187
  800.3 3.3 fusion.4
  803.6 31.1 %all-reduce.1 = (bf16[2048]{0:T(1024)(128)(2,1)S(1)}, bf16[2048]{0:T(1024)(128)(2,1)S(1)}) all-reduce(bf16[2048]{0:T(1024)(128)(2,1)S(1)} %get-tuple-element.17, bf16[2048]{0:T(1024)(128)(2,1)S(1)} %get-tuple-element.15), channel_id=1, replica_groups=mesh['ctx'=16,'mp'=8] {'ctx'}, use_global_device_ids=true, to_apply=%region_22.23 | all-reduce | flops 4096 | bytes 16384 | tf_op jit(solution)/shard_map/psum | solution.py:277
  835.9 6.8 fusion.7
  842.8 304.8 %all-reduce.13.cloned.1.call-done = (bf16[2048,256]{1,0:T(8,128)(2,1)}, bf16[2048,256]{1,0:T(8,128)(2,1)}, bf16[2048,256]{1,0:T(8,128)(2,1)}, bf16[256,2048]{1,0...) async-done(((bf16[2048,256]{1,0:T(8,128)(2,1)}, ...) | async-done | bytes 15269904 | tf_op jit(solution)/shard_map/psum | solution.py:278
  1147.6 2.9 convert_element_type.278
  1150.5 2.7 convert_element_type.280
  1162.9 2.6 convert_element_type.296
  1165.5 2.8 convert_element_type.298
  1168.2 2.6 convert_element_type.300
  (229 shorter events, 67.7 us)
Async XLA Ops:
  7.2 235.7 %copy-start = (bf16[3,176,2048]{2,1,0:T(8,128)(2,1)S(1)}, bf16[3,176,2048]{2,1,0:T(8,128)(2,1)}, u32[]{:S(2)}) copy-start(bf16[3,176,2048]{2,1,0:T(8,128)(2,1)} %param.31) | copy-start | bytes 6488068
  7.2 59.9 %all-gather.5.cloned.1.call-start = ((), (), s32[]{:S(2)}) async-start(), calls=%async_computation.3 | async-start | bytes 4456448 | tf_op jit(solution)/shard_map/all_gather | solution.py:156
  10.8 4.9 copy-start.57
  10.8 15.1 %copy-start.61 = (f32[512]{0:T(512)}, f32[512]{0:T(512)S(1)}, u32[]{:S(2)}) copy-start(f32[512]{0:T(512)S(1)} %fusion.72) | copy-start | bytes 6148
  25.9 80.9 %all-gather.3.cloned.1.call-start = ((), (), s32[]{:S(2)}) async-start(), calls=%async_computation.2 | async-start | bytes 4456448 | tf_op jit(solution)/shard_map/all_gather | solution.py:157
  29.3 206.0 %all-reduce.9.cloned.1.call-start = ((), (), s32[]{:S(2)}) async-start(), calls=%async_computation.4 | async-start | bytes 4194304 | tf_op jit(solution)/shard_map/psum | solution.py:163
  29.9 54.5 %copy-start.20 = (bf16[512,2,128]{2,0,1:T(8,128)(2,1)}, bf16[512,2,128]{2,0,1:T(8,128)(2,1)S(1)}, u32[]{:S(2)}) copy-start(bf16[512,2,128]{2,0,1:T(8,128)(2,1)S(1)} %fusion.33) | copy-start | bytes 786436
  100.1 24.0 %copy-start.22 = (bf16[256,2048]{1,0:T(8,128)(2,1)S(1)}, bf16[256,2048]{1,0:T(8,128)(2,1)}, u32[]{:S(2)}) copy-start(bf16[256,2048]{1,0:T(8,128)(2,1)} %param.23) | copy-start | bytes 3145732
  123.4 3.4 copy-start.69
  126.2 112.3 %copy-start.56 = (f32[2048]{0:T(1024)S(1)}, f32[2048]{0:T(1024)}, u32[]{:S(2)}) copy-start(f32[2048]{0:T(1024)} %param.24) | copy-start | bytes 24580
  126.2 265.1 %all-reduce.11.cloned.1.call-start = ((), (), s32[]{:S(2)}) async-start(), calls=%async_computation.5 | async-start | bytes 4194304 | tf_op jit(solution)/shard_map/psum | solution.py:213
  235.4 3.2 copy-start.2
  235.4 3.5 copy-start.9
  240.0 3.4 copy-start.6
  262.5 6.0 copy-start.12
  262.7 6.4 copy-start.14
  268.5 3.0 copy-start.49
  276.8 114.5 %copy-start.3 = (bf16[512,2048]{1,0:T(8,128)(2,1)S(1)}, bf16[512,2048]{1,0:T(8,128)(2,1)}, u32[]{:S(2)}) copy-start(bf16[512,2048]{1,0:T(8,128)(2,1)} %param.17) | copy-start | bytes 6291460
  276.8 114.5 %copy-start.46 = (f32[512,64]{0,1:T(8,128)S(1)}, f32[512,64]{0,1:T(8,128)}, u32[]{:S(2)}) copy-start(f32[512,64]{0,1:T(8,128)} %copy-done.45) | copy-start | bytes 393220
  276.8 114.5 %copy-start.68 = (f32[512]{0:T(512)S(1)}, f32[512]{0:T(512)}, u32[]{:S(2)}) copy-start(f32[512]{0:T(512)} %copy-done.67) | copy-start | bytes 6148
  276.8 114.5 %copy-start.70 = (f32[512]{0:T(512)S(1)}, f32[512]{0:T(512)}, u32[]{:S(2)}) copy-start(f32[512]{0:T(512)} %get-tuple-element.34) | copy-start | bytes 6148
  279.5 258.1 %reduce-scatter.3.cloned.1.call-start = ((), (), s32[]{:S(2)}) async-start(), calls=%async_computation.6 | async-start | bytes 4456448 | tf_op jit(solution)/shard_map/reduce_scatter | solution.py:229
  391.3 4.3 copy-start.66
  391.3 4.3 copy-start.10
  391.4 4.3 copy-start.17
  395.7 3.5 copy-start.23
  470.6 135.2 %reduce-scatter.5.cloned.1.call-start = ((), (), s32[]{:S(2)}) async-start(), calls=%async_computation.7 | async-start | bytes 4456448 | tf_op jit(solution)/shard_map/reduce_scatter | solution.py:235
  488.7 311.6 %all-reduce.15.cloned.1.call-start = ((), (), s32[]{:S(2)}) async-start(), calls=%async_computation.9 | async-start | bytes 8388608 | tf_op jit(solution)/shard_map/psum | solution.py:187
  489.3 3.2 copy-start.39
  489.3 3.2 copy-start.50
  549.9 4.3 copy-start.31
  549.9 4.3 copy-start.42
  611.7 3.3 copy-start.48
  611.7 535.9 %all-reduce.13.cloned.1.call-start = ((), (), s32[]{:S(2)}) async-start(), calls=%async_computation.8 | async-start | bytes 30539776 | tf_op jit(solution)/shard_map/psum | solution.py:278
  614.9 7.1 copy-start.8
  614.9 7.1 copy-start.44
  619.9 4.1 copy-start.53
  628.9 3.7 copy-start.32
  630.6 4.0 copy-start.54
  636.6 199.4 %copy-start.64 = (f32[512]{0:T(512)S(1)}, f32[512]{0:T(512)}, u32[]{:S(2)}) copy-start(f32[512]{0:T(512)} %copy-done.63) | copy-start | bytes 6148
  1147.6 5.6 copy-start.41
  1147.6 7.1 copy-start.40
  1150.5 5.8 copy-start.55
  1153.2 3.9 copy-start.36
  1154.7 4.3 copy-start.35
  1157.1 3.8 copy-start.34
  1159.0 3.8 copy-start.27
  1165.5 5.4 copy-start.1
  (31 other events, 57.5 us)
Sparse Core Ops, SparseCore 0:
  26.0 40.9 all-gather.4
  69.3 37.4 all-gather.2
  126.3 108.9 all-reduce.8
  279.6 111.6 all-reduce.10
  470.7 66.8 reduce-scatter.2
  539.8 65.8 reduce-scatter.4
  611.8 188.4 all-reduce.14
  805.0 342.6 all-reduce.12
where the time goes:
time: 1180 us
  waiting for transfers between devices  809 us (69%)
  matrix products  180 us (15%)
  other arithmetic  102 us (9%)
  blocking collectives  49.4 us (4%)
  local copies, waits for them, and re-layouts  21.3 us (2%)
  between operations  15 us (1%)
    psum x1, waiting for transfers between devices, on_device(): lax.psum(grad_w_query.astype(jnp.bfloat16), 'ctx').astype(jnp.float32)  305 us
    psum x1, waiting for transfers between devices, on_device(): lax.psum(moe_part.astype(jnp.bfloat16), 'mp').astype(jnp.float32)  164 us
    dot_general x33, matrix products, contract(): return jnp.einsum(pattern, left, right, preferred_element_type=jnp.float32)  157 us
    psum x1, waiting for transfers between devices, on_device(): lax.psum(grad_moe_in.astype(jnp.bfloat16), 'mp').astype(jnp.float32)  112 us
    psum x1, waiting for transfers between devices, on_device(): lax.psum(matmul(attended_low, w_out).astype(jnp.bfloat16), 'mp')  107 us
    reduce_scatter x1, waiting for transfers between devices, on_device(): lax.psum_scatter(value_part.reshape(v_every.shape[0], -1).astype(jnp.bflo...  48.8 us
    reduce_scatter x1, waiting for transfers between devices, on_device(): lax.psum_scatter(key_part.reshape(k_every.shape[0], -1).astype(jnp.bfloat...  33.2 us
    all_gather x1, waiting for transfers between devices, on_device(): lax.all_gather(k_rot.reshape(row_count, -1), 'ctx', axis=0, tiled=True)  32.6 us
  transfers between devices with their start and end apart: 8, of which 8 were waited for; matrix products, arithmetic and copies ran while one was open for 11% of the time, Pallas kernels for 0%

commit v1 on v0

v1 whole, which is shorter than its diff:
```python
import functools

import jax
import jax.numpy as jnp
from jax import lax
from jax.experimental import pallas as pl
from jax.experimental.pallas import tpu as pltpu
from jax.sharding import PartitionSpec as P

HD = 128
CAP = 32
EPSILON = 1e-06
ROPE_BASE = 10000.0
PRECISE = lax.Precision.HIGHEST
MESH = pl.DeviceIdType.MESH
BF = jnp.bfloat16
F32 = jnp.float32
D = 2048
R1 = 2640
R2 = 1088
VM = 60 * 2**20


def contract(pattern, left, right):
    return jnp.einsum(pattern, left, right, preferred_element_type=F32)


def exact_contract(pattern, left, right):
    return jnp.einsum(pattern, left, right, precision=PRECISE, preferred_element_type=F32)


def nt(a, b):
    return lax.dot_general(a, b, (((1,), (1,)), ((), ())), preferred_element_type=F32)


def nn(a, b):
    return lax.dot_general(a, b, (((1,), (0,)), ((), ())), preferred_element_type=F32)


def tn(a, b):
    return lax.dot_general(a, b, (((0,), (0,)), ((), ())), preferred_element_type=F32)


def rel8(i, d):
    ring = lax.rem(lax.div(i, 2) + d // 2 if isinstance(d, int) else lax.div(i, 2) + lax.div(d, 2), 4)
    pair = lax.rem(lax.rem(i, 2) + (d % 2 if isinstance(d, int) else lax.rem(d, 2)), 2)
    return ring * 2 + pair


def where_am_i():
    c = lax.axis_index("ctx")
    return c, lax.div(c, 2), lax.rem(c, 2), lax.axis_index("mp")


def remote(src, dst, ssem, rsem, dev):
    return pltpu.make_async_remote_copy(
        src_ref=src, dst_ref=dst, send_sem=ssem, recv_sem=rsem, device_id=dev, device_id_type=MESH
    )


def entry_barrier(ctx=True, mp=True):
    c, chip, core, m = where_am_i()
    bar = pltpu.get_barrier_semaphore()
    count = 0
    if ctx:
        pl.semaphore_signal(bar, inc=1, device_id={"ctx": chip * 2 + 1 - core}, device_id_type=MESH)
        count += 1
        for d in range(1, 8):
            pl.semaphore_signal(
                bar, inc=1, device_id={"ctx": rel8(chip, d) * 2 + core}, device_id_type=MESH
            )
            count += 1
    if mp:
        for d in range(1, 8):
            pl.semaphore_signal(bar, inc=1, device_id={"mp": rel8(m, d)}, device_id_type=MESH)
            count += 1
    pl.semaphore_wait(bar, count)


def mp_send_parts(parts, landing, ssem, rsem):
    m = lax.axis_index("mp")
    for d in range(1, 8):
        t = rel8(m, d)
        remote(parts.at[t], landing.at[m], ssem.at[d - 1], rsem.at[m], {"mp": t}).start()


def mp_send_same(src, landing, ssem, rsem):
    m = lax.axis_index("mp")
    for d in range(1, 8):
        t = rel8(m, d)
        remote(src, landing.at[m], ssem.at[d - 1], rsem.at[m], {"mp": t}).start()


def mp_wait_recv(landing, ssem, rsem, d):
    m = lax.axis_index("mp")
    t = rel8(m, d)
    remote(landing.at[t], landing.at[t], ssem.at[0], rsem.at[t], {"mp": t}).wait_recv()
    return t


def mp_wait_send(src, ssem):
    m = lax.axis_index("mp")
    for d in range(1, 8):
        remote(src, src, ssem.at[d - 1], ssem.at[d - 1], {"mp": rel8(m, d)}).wait_send()


def k1_kernel(
    sel, q, kv, tok, wout, gain,
    moe, mixed, lse, ot, kvall,
    st_m, st_l, st_a, att, parts, land,
    s_loc, s_sib, s_dir, s_rel, r_kv, s_mp, r_mp, s_ag, r_ag,
):
    c, chip, core, m = where_am_i()
    sib = chip * 2 + 1 - core
    entry_barrier()
    remote(kv, kvall.at[c], s_sib, r_kv.at[c], {"ctx": sib}).start()
    for d in range(1, 8):
        t = rel8(chip, d) * 2 + core
        remote(kv, kvall.at[c], s_dir.at[d - 1], r_kv.at[c], {"ctx": t}).start()
    own = pltpu.make_async_copy(kv, kvall.at[c], s_loc)
    own.start()

    st_m[...] = jnp.full_like(st_m, -1e30)
    st_l[...] = jnp.zeros_like(st_l)
    st_a[...] = jnp.zeros_like(st_a)

    def step(n, h, st, v):
        m0 = st_m[n, h]
        mn = jnp.maximum(m0, jnp.max(st, axis=0, keepdims=True))
        p = jnp.exp(st - mn)
        al = jnp.exp(m0 - mn)
        st_m[n, h] = mn
        st_l[n, h] = al * st_l[n, h] + jnp.sum(p, axis=0, keepdims=True)
        st_a[n, h] = al * st_a[n, h] + tn(v, p.astype(BF))

    def pick(s, h, st, v):
        m0 = jnp.where(s == 0, st_m[0, h], st_m[1, h])
        l0 = jnp.where(s == 0, st_l[0, h], st_l[1, h])
        a0 = st_a[s, h]
        mn = jnp.maximum(m0, jnp.max(st, axis=0, keepdims=True))
        p = jnp.exp(st - mn)
        al = jnp.exp(m0 - mn)
        l1 = al * l0 + jnp.sum(p, axis=0, keepdims=True)
        a1 = al * a0 + tn(v, p.astype(BF))
        for n in range(2):
            st_m[n, h] = jnp.where(s == n, mn, st_m[n, h])
            st_l[n, h] = jnp.where(s == n, l1, st_l[n, h])
            st_a[n, h] = jnp.where(s == n, a1, st_a[n, h])

    def block(j):
        s = sel[j]
        for h in range(2):
            cols = pl.ds(h * HD, HD)
            step(2, h, nt(kvall[j, 0, 0, :, cols], q[1, :, cols]), kvall[j, 1, 0, :, cols])
            ks = jnp.where(s == 0, kvall[j, 0, 0, :, cols], kvall[j, 0, 1, :, cols])
            vs = jnp.where(s == 0, kvall[j, 1, 0, :, cols], kvall[j, 1, 1, :, cols])
            pick(s, h, nt(ks, q[s, :, cols]), vs)

    tri = lax.broadcasted_iota(jnp.int32, (256, 256), 0) <= lax.broadcasted_iota(
        jnp.int32, (256, 256), 1
    )
    for h in range(2):
        cols = pl.ds(h * HD, HD)
        step(2, h, nt(kv[0, 0, :, cols], q[1, :, cols]), kv[1, 0, :, cols])
        for n in range(2):
            st = jnp.where(tri, nt(kv[0, n, :, cols], q[n, :, cols]), -1e30)
            step(n, h, st, kv[1, n, :, cols])

    def wait_block(j):
        remote(kvall.at[j], kvall.at[j], s_sib, r_kv.at[j], {"ctx": sib}).wait_recv()

    wait_block(sib)
    block(sib)

    def chips(i, carry):
        p = rel8(chip, i + 1)
        mine = p * 2 + core
        wait_block(mine)
        remote(kvall.at[mine], kvall.at[mine], s_rel.at[i], r_kv.at[mine], {"ctx": sib}).start()
        block(mine)
        other = p * 2 + 1 - core
        wait_block(other)
        block(other)
        return carry

    lax.fori_loop(0, 7, chips, 0)

    for h in range(2):
        for n in range(2):
            m0, l0, a0 = st_m[n, h], st_l[n, h], st_a[n, h]
            if n == 1:
                m2, l2, a2 = st_m[2, h], st_l[2, h], st_a[2, h]
                mn = jnp.maximum(m0, m2)
                e0, e2 = jnp.exp(m0 - mn), jnp.exp(m2 - mn)
                m0, l0, a0 = mn, e0 * l0 + e2 * l2, e0 * a0 + e2 * a2
            lse[n, h] = m0 + jnp.log(l0)
            o = a0 / l0
            ot[n, h] = o
            att[pl.ds(n * 256, 256), pl.ds(h * HD, HD)] = jnp.transpose(o).astype(BF)

    def out_cols(i, carry):
        cols = pl.ds(pl.multiple_of(i * 256, 256), 256)
        parts[:, :, cols] = nn(att[...], wout[:, cols]).reshape(8, 64, 256).astype(BF)
        return carry

    lax.fori_loop(0, 8, out_cols, 0)
    mp_send_parts(parts, land, s_mp, r_mp)
    total = tok[...].astype(F32) + parts[m].astype(F32)
    for d in range(1, 8):
        total = total + land[mp_wait_recv(land, s_mp, r_mp, d)].astype(F32)
    mixed[...] = total
    normed = total * lax.rsqrt(jnp.mean(total * total, axis=-1, keepdims=True) + EPSILON)
    moe[m] = (normed * gain[...]).astype(BF)
    mp_send_same(moe.at[m], moe, s_ag, r_ag)

    own.wait()
    remote(kv, kv, s_sib, s_sib, {"ctx": sib}).wait_send()
    for d in range(7):
        remote(kv, kv, s_dir.at[d], s_dir.at[d], {"ctx": sib}).wait_send()
        remote(kv, kv, s_rel.at[d], s_rel.at[d], {"ctx": sib}).wait_send()
    mp_wait_send(parts.at[0], s_mp)
    for d in range(1, 8):
        mp_wait_recv(moe, s_ag, r_ag, d)
    mp_wait_send(moe.at[0], s_ag)


def sds(shape, dtype):
    return jax.ShapeDtypeStruct(shape, dtype)


VMEM_SPEC = pl.BlockSpec(memory_space=pltpu.VMEM)
SMEM_SPEC = pl.BlockSpec(memory_space=pltpu.SMEM)
ANY_SPEC = pl.BlockSpec(memory_space=pl.ANY)
DMA = pltpu.SemaphoreType.DMA


def params(cid):
    return pltpu.CompilerParams(collective_id=cid, has_side_effects=True, vmem_limit_bytes=VM)


def attention_forward(sel, q, kv, tok_mine, w_out, gain):
    return pl.pallas_call(
        k1_kernel,
        name="attend_forward",
        out_shape=(
            sds((8, 64, D), BF),
            sds((64, D), F32),
            sds((2, 2, 1, 256), F32),
            sds((2, 2, HD, 256), F32),
            sds((16, 2, 2, 256, 256), BF),
        ),
        in_specs=[SMEM_SPEC] + [VMEM_SPEC] * 5,
        out_specs=(VMEM_SPEC,) * 5,
        scratch_shapes=[
            pltpu.VMEM((3, 2, 1, 256), F32),
            pltpu.VMEM((3, 2, 1, 256), F32),
            pltpu.VMEM((3, 2, HD, 256), F32),
            pltpu.VMEM((512, 256), BF),
            pltpu.VMEM((8, 64, D), BF),
            pltpu.VMEM((8, 64, D), BF),
            DMA, DMA, DMA((7,)), DMA((7,)), DMA((16,)),
            DMA((7,)), DMA((8,)), DMA((7,)), DMA((8,)),
        ],
        compiler_params=params(1),
    )(sel, q, kv, tok_mine, w_out, gain)


def w_sibling_sends(w, sibbuf, ssem, rsem):
    c, chip, core, m = where_am_i()
    sib = chip * 2 + 1 - core
    for k in range(8):
        cols = pl.ds(pl.multiple_of((2 * k + 1 - core) * HD, HD), HD)
        remote(w.at[:, cols], sibbuf.at[k], ssem.at[k], rsem.at[k], {"ctx": sib}).start()


def w_scatter(w, sibbuf, sums, land, ssem_sib, rsem_sib, ssem, rsem, rows, tile):
    c, chip, core, m = where_am_i()
    sib = chip * 2 + 1 - core

    def one(i, carry):
        k = rel8(chip, i + 1)
        remote(
            sibbuf.at[k], sibbuf.at[k], ssem_sib.at[0], rsem_sib.at[k], {"ctx": sib}
        ).wait_recv()
        cols = pl.ds(pl.multiple_of((2 * k + core) * HD, HD), HD)

        def add(r, carry):
            rr = pl.ds(pl.multiple_of(r * tile, 16), tile)
            sums[k, rr, :] = (w[rr, cols].astype(F32) + sibbuf[k, rr, :].astype(F32)).astype(BF)
            return carry

        lax.fori_loop(0, rows // tile, add, 0)

        @pl.when(i < 7)
        def _():
            remote(
                sums.at[k], land.at[chip], ssem.at[i], rsem.at[chip], {"ctx": k * 2 + core}
            ).start()

        return carry

    lax.fori_loop(0, 8, one, 0)


def w_total(sums, land, fin, ssem, rsem, rows, tile):
    c, chip, core, m = where_am_i()
    for d in range(1, 8):
        k = rel8(chip, d)
        remote(land.at[k], land.at[k], ssem.at[0], rsem.at[k], {"ctx": k * 2 + core}).wait_recv()

    def add(r, carry):
        rr = pl.ds(pl.multiple_of(r * tile, 16), tile)
        total = sums[chip, rr, :].astype(F32)
        for d in range(1, 8):
            total = total + land[rel8(chip, d), rr, :].astype(F32)
        fin[rr, :] = total.astype(BF)
        return carry

    lax.fori_loop(0, rows // tile, add, 0)


def w_scatter_drain(sibbuf, sums, ssem_sib, ssem):
    c, chip, core, m = where_am_i()
    sib = chip * 2 + 1 - core
    for k in range(8):
        remote(sibbuf.at[k], sibbuf.at[k], ssem_sib.at[k], ssem_sib.at[k], {"ctx": sib}).wait_send()
    for d in range(7):
        remote(sums.at[d], sums.at[d], ssem.at[d], ssem.at[d], {"ctx": sib}).wait_send()


def window(ref, j):
    return ref.at[:, pl.ds(pl.multiple_of(j * HD, HD), HD)]


def w_gather_start(fin, out, s_loc, s_sib, s_dir, rsem):
    c, chip, core, m = where_am_i()
    sib = chip * 2 + 1 - core
    for d in range(1, 8):
        t = rel8(chip, d) * 2 + core
        remote(fin, window(out, c), s_dir.at[d - 1], rsem.at[c], {"ctx": t}).start()
    remote(fin, window(out, c), s_sib, rsem.at[c], {"ctx": sib}).start()
    pltpu.make_async_copy(fin, window(out, c), s_loc).start()


def w_gather_relay(out, s_rel, rsem, i):
    c, chip, core, m = where_am_i()
    sib = chip * 2 + 1 - core
    j = rel8(chip, i + 1) * 2 + core
    win = window(out, j)
    remote(win, win, s_rel.at[i], rsem.at[j], {"ctx": sib}).wait_recv()
    remote(win, win, s_rel.at[i], rsem.at[j], {"ctx": sib}).start()


def w_gather_drain(fin, out, s_loc, s_sib, s_dir, s_rel, rsem):
    c, chip, core, m = where_am_i()
    sib = chip * 2 + 1 - core
    pltpu.make_async_copy(fin, window(out, c), s_loc).wait()
    remote(fin, fin, s_sib, s_sib, {"ctx": sib}).wait_send()
    for d in range(7):
        remote(fin, fin, s_dir.at[d], s_dir.at[d], {"ctx": sib}).wait_send()
        remote(fin, fin, s_rel.at[d], s_rel.at[d], {"ctx": sib}).wait_send()
    remote(window(out, sib), window(out, sib), s_sib, rsem.at[sib], {"ctx": sib}).wait_recv()
    for d in range(1, 8):
        j = rel8(chip, d) * 2 + 1 - core
        remote(window(out, j), window(out, j), s_sib, rsem.at[j], {"ctx": sib}).wait_recv()


def k2_kernel(
    gmi, gate_part, mixed, cot, gain, w_router, probs, slots, w1,
    g_attn, g_mixed, gain_part, gate_sum, fin,
    land, gate_land, sibbuf, sums, wland,
    s_mp, r_mp, s_gate, r_gate, s_ag, r_ag, s_wsib, r_wsib, s_w, r_w,
):
    c, chip, core, m = where_am_i()
    entry_barrier()
    mp_send_parts(gmi, land, s_mp, r_mp)
    mp_send_same(gate_part, gate_land, s_gate, r_gate)
    w_sibling_sends(w1, sibbuf, s_wsib, r_wsib)
    w_scatter(w1, sibbuf, sums, wland, s_wsib, r_wsib, s_w, r_w, R1, 528)

    gate = gate_part[...]
    for d in range(1, 8):
        gate = gate + gate_land[mp_wait_recv(gate_land, s_gate, r_gate, d)]
    gate_sum[...] = gate
    lane = lax.broadcasted_iota(jnp.int32, (HD, 64), 0)
    col = lax.broadcasted_iota(jnp.int32, (HD, 64), 1)
    member = jnp.where((lane >= col * CAP) & (lane < (col + 1) * CAP) & (col < 3), 1.0, 0.0)
    grad_probs = lax.dot_general(
        slots[...] * gate, member, (((1,), (0,)), ((), ())),
        precision=PRECISE, preferred_element_type=F32,
    )
    pr = probs[...]
    logits = (pr * (grad_probs - jnp.sum(grad_probs * pr, axis=-1, keepdims=True))).astype(BF)

    total = nt(logits, w_router[...]) + gmi[m].astype(F32)
    for d in range(1, 8):
        total = total + land[mp_wait_recv(land, s_mp, r_mp, d)].astype(F32)
    mx = mixed[...]
    n = lax.rsqrt(jnp.mean(mx * mx, axis=-1, keepdims=True) + EPSILON)
    gain_part[...] = jnp.sum(total * mx * n, axis=0, keepdims=True)
    gg = total * gain[...]
    gm = cot[...].astype(F32) + n * gg - mx * (n * n * n) * jnp.mean(gg * mx, axis=-1, keepdims=True)
    g_mixed[...] = gm
    g_attn[m] = gm.astype(BF)
    mp_send_same(g_attn.at[m], g_attn, s_ag, r_ag)

    w_total(sums, wland, fin, s_w, r_w, R1, 528)
    w_scatter_drain(sibbuf, sums, s_wsib, s_w)
    mp_wait_send(gmi.at[0], s_mp)
    mp_wait_send(gate_part, s_gate)
    for d in range(1, 8):
        mp_wait_recv(g_attn, s_ag, r_ag, d)
    mp_wait_send(g_attn.at[0], s_ag)


def second_norm_backward(gmi, gate_part, mixed, cot, gain, w_router, probs, slots, w1):
    return pl.pallas_call(
        k2_kernel,
        name="second_norm_backward",
        out_shape=(
            sds((8, 64, D), BF),
            sds((64, D), F32),
            sds((1, D), F32),
            sds((1, HD), F32),
            sds((R1, HD), BF),
        ),
        in_specs=[VMEM_SPEC] * 9,
        out_specs=(VMEM_SPEC,) * 5,
        scratch_shapes=[
            pltpu.VMEM((8, 64, D), BF),
            pltpu.VMEM((8, 1, HD), F32),
            pltpu.VMEM((8, R1, HD), BF),
            pltpu.VMEM((8, R1, HD), BF),
            pltpu.VMEM((8, R1, HD), BF),
            DMA((7,)), DMA((8,)), DMA((7,)), DMA((8,)), DMA((7,)), DMA((8,)),
            DMA((8,)), DMA((8,)), DMA((7,)), DMA((8,)),
        ],
        compiler_params=params(2),
    )(gmi, gate_part, mixed, cot, gain, w_router, probs, slots, w1)


def k3_kernel(
    sel, q, kvall, lse, ot, g_attn, wout, moe_part, mixed, fin,
    output, w1, dq, dkv,
    do, delta, dqt, cur, to_sib, from_sib, to_far, from_far, oland,
    s_sib, r_sib, s_far, r_far, s_mp, r_mp, s_ag, r_ag, s_loc, s_wsib, s_wdir, s_wrel, r_w,
):
    c, chip, core, m = where_am_i()
    sib = chip * 2 + 1 - core
    entry_barrier()
    mp_send_parts(moe_part, oland, s_mp, r_mp)
    w_gather_start(fin, w1, s_loc, s_wsib, s_wdir, r_w)

    g_att = nt(g_attn[...], wout[...])
    for n in range(2):
        for h in range(2):
            piece = g_att[n * 256 : n * 256 + 256, h * HD : h * HD + HD].astype(BF)
            do[n, h] = piece
            dot_t = jnp.transpose(piece.astype(F32))
            delta[n, h] = jnp.sum(dot_t * ot[n, h], axis=0, keepdims=True)
    dqt[...] = jnp.zeros_like(dqt)

    def terms(h, k, v, qq, dd, ls, de, mask):
        p = jnp.exp(nt(k, qq) - ls)
        if mask is not None:
            p = jnp.where(mask, p, 0.0)
        ds = (p * (nt(v, dd) - de)).astype(BF)
        return nn(ds, qq), nn(p.astype(BF), dd), tn(k, ds)

    def block(j, store):
        s = sel[j]
        for h in range(2):
            cols = pl.ds(h * HD, HD)
            dk0, dv0, dq0 = terms(
                h, kvall[j, 0, 0, :, cols], kvall[j, 1, 0, :, cols], q[1, :, cols], do[1, h],
                lse[1, h], delta[1, h], None,
            )
            dqt[2, h] += dq0
            ls = jnp.where(s == 0, lse[0, h], lse[1, h])
            de = jnp.where(s == 0, delta[0, h], delta[1, h])
            dk1, dv1, dq1 = terms(
                h, kvall[j, 0, s, :, cols], kvall[j, 1, s, :, cols], q[s, :, cols], do[s, h],
                ls, de, None,
            )
            for n in range(2):
                dqt[n, h] += jnp.where(s == n, dq1, 0.0)
            store(0, 0, cols, dk0 + jnp.where(s == 0, dk1, 0.0))
            store(1, 0, cols, dv0 + jnp.where(s == 0, dv1, 0.0))
            store(0, 1, cols, jnp.where(s == 1, dk1, 0.0))
            store(1, 1, cols, jnp.where(s == 1, dv1, 0.0))

    def finish(i):
        k = rel8(chip, i + 1)
        remote(from_sib.at[k], from_sib.at[k], s_sib.at[0], r_sib.at[k], {"ctx": sib}).wait_recv()
        for a in range(2):
            for n in range(2):
                to_far[k, a, n] = (to_far[k, a, n].astype(F32) + from_sib[k, a, n].astype(F32)).astype(BF)
        remote(to_far.at[k], from_far.at[chip], s_far.at[i], r_far.at[chip], {"ctx": k * 2 + core}).start()

    def chips(i, carry):
        k = rel8(chip, i + 1)

        def to_sibling(a, n, cols, val):
            to_sib[k, a, n, :, cols] = val.astype(BF)

        block(k * 2 + 1 - core, to_sibling)
        remote(to_sib.at[k], from_sib.at[k], s_sib.at[k], r_sib.at[k], {"ctx": sib}).start()

        def to_chip(a, n, cols, val):
            to_far[k, a, n, :, cols] = val.astype(BF)

        block(k * 2 + core, to_chip)

        @pl.when(i > 0)
        def _():
            finish(i - 1)

        return carry

    lax.fori_loop(0, 7, chips, 0)

    def to_sibling(a, n, cols, val):
        to_sib[chip, a, n, :, cols] = val.astype(BF)

    block(sib, to_sibling)
    remote(to_sib.at[chip], from_sib.at[chip], s_sib.at[chip], r_sib.at[chip], {"ctx": sib}).start()
    finish(6)

    tri = lax.broadcasted_iota(jnp.int32, (256, 256), 0) <= lax.broadcasted_iota(
        jnp.int32, (256, 256), 1
    )
    for h in range(2):
        cols = pl.ds(h * HD, HD)
        k0, v0 = kvall[c, 0, 0, :, cols], kvall[c, 1, 0, :, cols]
        dk0, dv0, dq0 = terms(h, k0, v0, q[1, :, cols], do[1, h], lse[1, h], delta[1, h], None)
        dqt[2, h] += dq0
        for n in range(2):
            kn, vn = kvall[c, 0, n, :, cols], kvall[c, 1, n, :, cols]
            dk1, dv1, dq1 = terms(h, kn, vn, q[n, :, cols], do[n, h], lse[n, h], delta[n, h], tri)
            dqt[n, h] += dq1
            cur[0, n, :, cols] = dk0 + dk1 if n == 0 else dk1
            cur[1, n, :, cols] = dv0 + dv1 if n == 0 else dv1
    for h in range(2):
        dq[0, :, pl.ds(h * HD, HD)] = jnp.transpose(dqt[0, h])
        dq[1, :, pl.ds(h * HD, HD)] = jnp.transpose(dqt[1, h] + dqt[2, h])

    total = mixed[...] + moe_part[m].astype(F32)
    for d in range(1, 8):
        total = total + oland[mp_wait_recv(oland, s_mp, r_mp, d)].astype(F32)
    output[m] = total.astype(BF)
    mp_send_same(output.at[m], output, s_ag, r_ag)

    def relay(i, carry):
        w_gather_relay(w1, s_wrel, r_w, i)
        return carry

    lax.fori_loop(0, 7, relay, 0)

    remote(from_sib.at[chip], from_sib.at[chip], s_sib.at[0], r_sib.at[chip], {"ctx": sib}).wait_recv()
    for d in range(1, 8):
        k = rel8(chip, d)
        remote(from_far.at[k], from_far.at[k], s_sib.at[0], r_far.at[k], {"ctx": sib}).wait_recv()

    def add(i, carry):
        a, n = lax.div(i, 2), lax.rem(i, 2)
        t = cur[a, n] + from_sib[chip, a, n].astype(F32)
        for d in range(1, 8):
            t = t + from_far[rel8(chip, d), a, n].astype(F32)
        dkv[a, n] = t
        return carry

    lax.fori_loop(0, 4, add, 0)

    for k in range(8):
        remote(to_sib.at[k], to_sib.at[k], s_sib.at[k], s_sib.at[k], {"ctx": sib}).wait_send()
    for d in range(7):
        remote(to_far.at[d], to_far.at[d], s_far.at[d], s_far.at[d], {"ctx": sib}).wait_send()
    mp_wait_send(moe_part.at[0], s_mp)
    for d in range(1, 8):
        mp_wait_recv(output, s_ag, r_ag, d)
    mp_wait_send(output.at[0], s_ag)
    w_gather_drain(fin, w1, s_loc, s_wsib, s_wdir, s_wrel, r_w)


def attention_backward(sel, q, kvall, lse, ot, g_attn, w_out, moe_part, mixed, fin):
    return pl.pallas_call(
        k3_kernel,
        name="attend_backward",
        out_shape=(
            sds((8, 64, D), BF),
            sds((R1, D), BF),
            sds((2, 256, 256), F32),
            sds((2, 2, 256, 256), F32),
        ),
        in_specs=[SMEM_SPEC] + [VMEM_SPEC] * 9,
        out_specs=(VMEM_SPEC, ANY_SPEC, VMEM_SPEC, VMEM_SPEC),
        scratch_shapes=[
            pltpu.VMEM((2, 2, 256, HD), BF),
            pltpu.VMEM((2, 2, 1, 256), F32),
            pltpu.VMEM((3, 2, HD, 256), F32),
            pltpu.VMEM((2, 2, 256, 256), F32),
            pltpu.VMEM((8, 2, 2, 256, 256), BF),
            pltpu.VMEM((8, 2, 2, 256, 256), BF),
            pltpu.VMEM((8, 2, 2, 256, 256), BF),
            pltpu.VMEM((8, 2, 2, 256, 256), BF),
            pltpu.VMEM((8, 64, D), BF),
            DMA((8,)), DMA((8,)), DMA((7,)), DMA((8,)),
            DMA((7,)), DMA((8,)), DMA((7,)), DMA((8,)),
            DMA, DMA, DMA((7,)), DMA((7,)), DMA((16,)),
        ],
        compiler_params=params(3),
    )(sel, q, kvall, lse, ot, g_attn, w_out, moe_part, mixed, fin)


def k4_kernel(
    gni, tok, g_mixed, gain, gain_moe_part, w2,
    g_tokens, w2out, gains,
    land, sibbuf, sums, wland, fin, gmine, gland, gpart, gfar,
    s_mp, r_mp, s_ag, r_ag, s_wsib, r_wsib, s_w, r_w, s_loc, s_gsib, s_gdir, s_grel, r_g,
    s_gm, r_gm, s_gs, r_gs, s_gc, r_gc,
):
    c, chip, core, m = where_am_i()
    sib = chip * 2 + 1 - core
    entry_barrier()
    mp_send_parts(gni, land, s_mp, r_mp)
    w_sibling_sends(w2, sibbuf, s_wsib, r_wsib)
    w_scatter(w2, sibbuf, sums, wland, s_wsib, r_wsib, s_w, r_w, R2, 544)

    total = gni[m].astype(F32)
    for d in range(1, 8):
        total = total + land[mp_wait_recv(land, s_mp, r_mp, d)].astype(F32)
    src = tok[...].astype(F32)
    n = lax.rsqrt(jnp.mean(src * src, axis=-1, keepdims=True) + EPSILON)
    gg = total * gain[...]
    gs = n * gg - src * (n * n * n) * jnp.mean(gg * src, axis=-1, keepdims=True)
    g_tokens[m] = (g_mixed[...] + gs).astype(BF)
    mp_send_same(g_tokens.at[m], g_tokens, s_ag, r_ag)
    gmine[pl.ds(0, 1), :] = gain_moe_part[...]
    gmine[pl.ds(1, 1), :] = jnp.sum(total * src * n, axis=0, keepdims=True)
    mp_send_same(gmine, gland, s_gm, r_gm)

    w_total(sums, wland, fin, s_w, r_w, R2, 544)
    w_gather_start(fin, w2out, s_loc, s_gsib, s_gdir, r_g)

    gsum = gmine[...]
    for d in range(1, 8):
        gsum = gsum + gland[mp_wait_recv(gland, s_gm, r_gm, d)]
    gpart[0] = gsum
    remote(gpart.at[0], gpart.at[1], s_gs, r_gs, {"ctx": sib}).start()
    remote(gpart.at[0], gpart.at[1], s_gs, r_gs, {"ctx": sib}).wait_recv()
    gpart[2] = gpart[0] + gpart[1]
    for d in range(1, 8):
        k = rel8(chip, d)
        remote(gpart.at[2], gfar.at[chip], s_gc.at[d - 1], r_gc.at[chip], {"ctx": k * 2 + core}).start()
    gfar[chip] = gpart[2]
    for d in range(1, 8):
        k = rel8(chip, d)
        remote(gfar.at[k], gfar.at[k], s_gs, r_gc.at[k], {"ctx": sib}).wait_recv()
    gsum = gfar[0]
    for k in range(1, 8):
        gsum = gsum + gfar[k]
    gains[...] = gsum

    def relay(i, carry):
        w_gather_relay(w2out, s_grel, r_g, i)
        return carry

    lax.fori_loop(0, 7, relay, 0)
    remote(gpart.at[0], gpart.at[1], s_gs, r_gs, {"ctx": sib}).wait_send()
    for d in range(7):
        remote(gpart.at[2], gpart.at[2], s_gc.at[d], s_gc.at[d], {"ctx": sib}).wait_send()
    mp_wait_send(gmine, s_gm)
    w_scatter_drain(sibbuf, sums, s_wsib, s_w)
    mp_wait_send(gni.at[0], s_mp)
    for d in range(1, 8):
        mp_wait_recv(g_tokens, s_ag, r_ag, d)
    mp_wait_send(g_tokens.at[0], s_ag)
    w_gather_drain(fin, w2out, s_loc, s_gsib, s_gdir, s_grel, r_g)


def first_norm_backward(gni, tok, g_mixed, gain, gain_moe_part, w2):
    return pl.pallas_call(
        k4_kernel,
        name="first_norm_backward",
        out_shape=(sds((8, 64, D), BF), sds((R2, D), BF), sds((2, D), F32)),
        in_specs=[VMEM_SPEC] * 6,
        out_specs=(VMEM_SPEC, ANY_SPEC, VMEM_SPEC),
        scratch_shapes=[
            pltpu.VMEM((8, 64, D), BF),
            pltpu.VMEM((8, R2, HD), BF),
            pltpu.VMEM((8, R2, HD), BF),
            pltpu.VMEM((8, R2, HD), BF),
            pltpu.VMEM((R2, HD), BF),
            pltpu.VMEM((2, D), F32),
            pltpu.VMEM((8, 2, D), F32),
            pltpu.VMEM((3, 2, D), F32),
            pltpu.VMEM((8, 2, D), F32),
            DMA((7,)), DMA((8,)), DMA((7,)), DMA((8,)),
            DMA((8,)), DMA((8,)), DMA((7,)), DMA((8,)),
            DMA, DMA, DMA((7,)), DMA((7,)), DMA((16,)),
            DMA((7,)), DMA((8,)), DMA, DMA, DMA((7,)), DMA((8,)),
        ],
        compiler_params=params(4),
    )(gni, tok, g_mixed, gain, gain_moe_part, w2)


def rms_norm(values, gain_vec):
    return (
        values * lax.rsqrt(jnp.mean(values * values, axis=-1, keepdims=True) + EPSILON) * gain_vec
    )


def swiglu(gate_vals, up_vals):
    return jax.nn.silu(gate_vals) * up_vals


def rotate(values, angle_cos, angle_sin):
    half_dim = values.shape[-1] // 2
    first_half = values[..., :half_dim]
    second_half = values[..., half_dim:]
    return jnp.concatenate(
        [
            first_half * angle_cos - second_half * angle_sin,
            second_half * angle_cos + first_half * angle_sin,
        ],
        axis=-1,
    )


def angles(position, head_dim):
    index_range = jnp.arange(head_dim // 2, dtype=F32)
    inverse = ROPE_BASE ** (-2.0 * index_range / head_dim)
    phase = position.astype(F32)[:, None] * inverse[None, :]
    return (jnp.cos(phase)[:, None, :], jnp.sin(phase)[:, None, :])


def dispatch_table(expert_ids, held_count, slot_count):
    chosen = jnp.any(
        expert_ids[:, :, None] == jnp.arange(held_count, dtype=jnp.int32)[None, None, :], axis=1
    )
    held_flag = chosen.astype(jnp.int32)
    slot_index = jnp.cumsum(held_flag, axis=0) - 1
    placed = chosen[:, :, None] & (
        slot_index[:, :, None] == jnp.arange(slot_count, dtype=jnp.int32)[None, None, :]
    )
    return placed.astype(F32)


def on_device(
    tokens, cotangent, gain_attn, w_query, w_key, w_value, w_out, gain_moe, w_router,
    shared_gate, shared_up, shared_down, expert_gate, expert_up, expert_down, expert_ids, pair_order,
):
    rows = tokens.shape[0]
    head_shape = (rows, 2, HD)
    member = lax.axis_index("ctx")
    mine = lax.axis_index("mp")
    pair = lax.dynamic_index_in_dim(pair_order, member, keepdims=False)
    within = jnp.arange(rows, dtype=jnp.int32)
    pos = jnp.where(within < 256, pair * 256 + within, (31 - pair) * 256 + within - 256)
    cos_mine, sin_mine = angles(pos, HD)
    sel = jnp.where(pair_order < pair, 0, 1).astype(jnp.int32)
    scale = HD ** (-0.5)
    source = tokens.astype(F32)
    normed_low = rms_norm(source, gain_attn).astype(BF)
    q_lin = nn(normed_low, w_query).reshape(head_shape)
    k_lin = nn(normed_low, w_key).reshape(head_shape)
    v_low = nn(normed_low, w_value).astype(BF)
    q_rot = (rotate(q_lin, cos_mine, sin_mine) * scale).astype(BF).reshape(2, 256, 256)
    k_rot = rotate(k_lin, cos_mine, sin_mine).astype(BF).reshape(2, 256, 256)
    kv = jnp.stack([k_rot, v_low.reshape(2, 256, 256)])
    tok_mine = lax.dynamic_slice_in_dim(tokens, mine * 64, 64)
    cot_mine = lax.dynamic_slice_in_dim(cotangent, mine * 64, 64)
    moe_all, mixed, lse, ot, kvall = attention_forward(
        sel, q_rot, kv, tok_mine, w_out, gain_moe[None]
    )
    moe_low = moe_all.reshape(rows, D)
    attended_low = ot.transpose(0, 3, 1, 2).reshape(rows, 256).astype(BF)

    router_probs = jax.nn.softmax(nn(moe_low, w_router), axis=-1)
    shared_g = nn(moe_low, shared_gate)
    shared_u = nn(moe_low, shared_up)
    shared_act, shared_pull = jax.vjp(swiglu, shared_g, shared_u)
    shared_hidden = shared_act.astype(BF)
    held = expert_gate.shape[0]
    slot_table = dispatch_table(expert_ids, held, CAP)
    table_low = slot_table.astype(BF)
    expert_in = contract("tec,td->ecd", table_low, moe_low).astype(BF)
    gate_slot = exact_contract("tec,te->ec", slot_table, router_probs[:, :held])
    expert_g = contract("ecd,edf->ecf", expert_in, expert_gate)
    expert_u = contract("ecd,edf->ecf", expert_in, expert_up)
    expert_act, expert_pull = jax.vjp(swiglu, expert_g, expert_u)
    expert_hidden = expert_act.astype(BF)
    expert_part = contract("ecf,efd->ecd", expert_hidden, expert_down)
    gated_part = gate_slot[:, :, None] * expert_part
    moe_part = nn(shared_hidden, shared_down) + exact_contract("tec,ecd->td", slot_table, gated_part)
    moe_part = moe_part.astype(BF).reshape(8, 64, D)

    grad_shared_hidden = contract("td,fd->tf", cotangent, shared_down)
    g_shared_g, g_shared_u = shared_pull(grad_shared_hidden)
    g_sg = g_shared_g.astype(BF)
    g_su = g_shared_u.astype(BF)
    grad_moe_in = contract("tf,df->td", g_sg, shared_gate) + contract("tf,df->td", g_su, shared_up)
    grad_slot = contract("tec,td->ecd", table_low, cotangent)
    grad_expert_out = (gate_slot[:, :, None] * grad_slot).astype(BF)
    gate_grad_part = jnp.sum(grad_slot * expert_part, axis=-1)
    grad_expert_hidden = contract("ecd,efd->ecf", grad_expert_out, expert_down)
    g_expert_g, g_expert_u = expert_pull(grad_expert_hidden)
    g_eg = g_expert_g.astype(BF)
    g_eu = g_expert_u.astype(BF)
    grad_expert_in = contract("ecf,edf->ecd", g_eg, expert_gate) + contract(
        "ecf,edf->ecd", g_eu, expert_up
    )
    grad_moe_in = grad_moe_in + exact_contract("tec,ecd->td", slot_table, grad_expert_in)
    grad_moe_in = grad_moe_in.astype(BF).reshape(8, 64, D)
    w1 = jnp.concatenate(
        [
            contract("tf,td->fd", g_sg, moe_low).astype(BF),
            contract("tf,td->fd", g_su, moe_low).astype(BF),
            contract("tf,td->fd", shared_hidden, cotangent).astype(BF),
            contract("ecf,ecd->efd", g_eg, expert_in).astype(BF).reshape(-1, D),
            contract("ecf,ecd->efd", g_eu, expert_in).astype(BF).reshape(-1, D),
            contract("ecf,ecd->efd", expert_hidden, grad_expert_out).astype(BF).reshape(-1, D),
        ]
    )

    gate_part = jnp.pad(gate_grad_part.reshape(1, -1), ((0, 0), (0, HD - held * CAP)))
    slots = jnp.pad(slot_table.reshape(rows, -1), ((0, 0), (0, HD - held * CAP)))
    slots_mine = lax.dynamic_slice_in_dim(slots, mine * 64, 64)
    probs_mine = lax.dynamic_slice_in_dim(router_probs, mine * 64, 64)
    g_attn, g_mixed, gain_moe_part, gate_sum, fin = second_norm_backward(
        grad_moe_in, gate_part, mixed, cot_mine, gain_moe[None], w_router, probs_mine, slots_mine, w1
    )
    grad_held = exact_contract(
        "tec,ec->te", slot_table, gate_sum[0, : held * CAP].reshape(held, CAP)
    )
    grad_probs = jnp.pad(grad_held, ((0, 0), (0, router_probs.shape[1] - held)))
    g_logits = (
        router_probs * (grad_probs - jnp.sum(grad_probs * router_probs, axis=-1, keepdims=True))
    ).astype(BF)

    g_attn = g_attn.reshape(rows, D)
    output, w1, dq, dkv = attention_backward(
        sel, q_rot, kvall, lse, ot, g_attn, w_out, moe_part, mixed, fin
    )
    grad_q_lin = (
        rotate(dq.reshape(head_shape) * scale, cos_mine, -sin_mine).reshape(rows, -1).astype(BF)
    )
    grad_k_lin = (
        rotate(dkv[0].reshape(head_shape), cos_mine, -sin_mine).reshape(rows, -1).astype(BF)
    )
    grad_v_lin = dkv[1].reshape(rows, -1).astype(BF)
    grad_normed = (
        contract("tk,dk->td", grad_q_lin, w_query)
        + contract("tk,dk->td", grad_k_lin, w_key)
        + contract("tk,dk->td", grad_v_lin, w_value)
    )
    grad_normed = grad_normed.astype(BF).reshape(8, 64, D)
    w2 = jnp.concatenate(
        [
            contract("tk,td->kd", grad_q_lin, normed_low).astype(BF),
            contract("tk,td->kd", grad_k_lin, normed_low).astype(BF),
            contract("tk,td->kd", grad_v_lin, normed_low).astype(BF),
            contract("tk,td->kd", attended_low, g_attn).astype(BF),
            contract("te,td->ed", g_logits, moe_low).astype(BF),
        ]
    )
    g_tokens, w2, gains = first_norm_backward(
        grad_normed, tok_mine, g_mixed, gain_attn[None], gain_moe_part, w2
    )
    w1 = w1.astype(F32)
    w2 = w2.astype(F32)
    return (
        output.reshape(rows, D),
        g_tokens.reshape(rows, D),
        gains[1],
        w2[:256].T,
        w2[256:512].T,
        w2[512:768].T,
        w2[768:1024],
        gains[0],
        w2[1024:].T,
        w1[:352].T,
        w1[352:704].T,
        w1[704:1056],
        w1[1056:1584].reshape(3, 176, D).transpose(0, 2, 1),
        w1[1584:2112].reshape(3, 176, D).transpose(0, 2, 1),
        w1[2112:].reshape(3, 176, D),
    )


def solution(mesh):
    in_specs = (
        P("ctx", None),
        P("ctx", None),
        P(),
        P(None, "mp"),
        P(None, "mp"),
        P(None, "mp"),
        P("mp", None),
        P(),
        P(),
        P(None, "mp"),
        P(None, "mp"),
        P("mp", None),
        P(None, None, "mp"),
        P(None, None, "mp"),
        P(None, "mp", None),
        P("ctx", None),
        P(),
    )
    out_specs = (
        P("ctx", None),
        P("ctx", None),
        P(),
        P(None, "mp"),
        P(None, "mp"),
        P(None, "mp"),
        P("mp", None),
        P(),
        P(),
        P(None, "mp"),
        P(None, "mp"),
        P("mp", None),
        P(None, None, "mp"),
        P(None, None, "mp"),
        P(None, "mp", None),
    )
    return jax.shard_map(
        on_device, mesh=mesh, in_specs=in_specs, out_specs=out_specs, check_vma=False
    )
```

time: 1180 us -> 740 us (0.63)
  waiting for transfers between devices: 809 us -> 0 us
  Pallas kernels: 0 us -> 562 us
  matrix products: 180 us -> 56.9 us
  other arithmetic: 102 us -> 40.4 us
  blocking collectives: 49.4 us -> 0 us
  local copies, waits for them, and re-layouts: 21.3 us -> 65.1 us
  between operations: 15 us -> 2.97 us
    psum x4 -> x0, waiting for transfers between devices: 687 us -> none  [the longest x1 305 us: on_device(): lax.psum(grad_w_query.astype(jnp.bfloat16), 'ctx').astype(jnp.float32)]
    pallas_call x0 -> x4, Pallas kernels: none -> 562 us  [the longest x1 169 us: attention_backward(): pl.pallas_call(k3_kernel, name='attend_backward', out_shape=(sds((8, 64,...]
    dot_general x41 -> x32, matrix products: 175 us -> 52.7 us  [the longest x25 38.1 us: contract(): return jnp.einsum(pattern, left, right, preferred_element_type=F32)]
    reduce_scatter x2 -> x0, waiting for transfers between devices: 81.9 us -> none  [the longest x1 48.8 us: on_device(): lax.psum_scatter(value_part.reshape(v_every.shape[0], -1).astype(jnp.bflo...]
    psum x2 -> x0, blocking collectives: 49.4 us -> none  [the longest x1 31.1 us: on_device(): lax.psum(grad_gain_attn.astype(jnp.bfloat16), 'ctx').astype(jnp.float32)]
    convert_element_type x18 -> x5, other arithmetic: 61.7 us -> 18.3 us  [the longest x1 14.2 us: on_device(): w1 = w1.astype(F32)]
    all_gather x2 -> x0, waiting for transfers between devices: 39.3 us -> none  [the longest x1 32.6 us: on_device(): lax.all_gather(k_rot.reshape(row_count, -1), 'ctx', axis=0, tiled=True)]
    reduce_sum x4 -> x2, other arithmetic: 19.7 us -> 1.48 us  [the longest x1 1.18 us: on_device(): router_probs = jax.nn.softmax(nn(moe_low, w_router), axis=-1)]
  transfers between devices with their start and end apart: 8 -> 0, of which waited for: 8 -> 0; matrix products, arithmetic and copies ran while one was open for 11% -> 0% of each run, Pallas kernels for 0% -> 0%
where the time goes in v1:
time: 740 us; the launch traced here: 727 us
  Pallas kernels  562 us (76%)
  local copies, waits for them, and re-layouts  65.1 us (9%)
  matrix products  56.9 us (8%)
  other arithmetic  40.4 us (5%)
    pallas_call x1, Pallas kernels, attention_backward(): pl.pallas_call(k3_kernel, name='attend_backward', out_shape=(sds((8, 64,...  169 us
    pallas_call x1, Pallas kernels, attention_forward(): pl.pallas_call(k1_kernel, name='attend_forward', out_shape=(sds((8, 64, D...  148 us
    pallas_call x1, Pallas kernels, second_norm_backward(): pl.pallas_call(k2_kernel, name='second_norm_backward', out_shape=(sds((8,...  130 us
    pallas_call x1, Pallas kernels, first_norm_backward(): pl.pallas_call(k4_kernel, name='first_norm_backward', out_shape=(sds((8,...  115 us
    dot_general x25, matrix products, contract(): return jnp.einsum(pattern, left, right, preferred_element_type=F32)  38.1 us
    unnamed x125, local copies, waits for them, and re-layouts  25.8 us

profile of v1, /device:TPU:1, one launch (start us, length us, event | category | flops | bytes accessed | tf_op | source)
XLA Modules:
  0.0 727.1 jit_solution(6734513074364063885)
XLA Ops:
  2.1 1.8 compare_select_fusion.sel
  3.9 2.1 fusion
  6.0 2.8 fusion.71
  10.7 1.8 fusion.63
  12.5 2.9 fusion.73
  16.2 1.9 copy.86
  18.2 1.9 copy.87
  20.1 3.1 subtract_convert_fusion.2
  24.8 2.7 convolution_convert_fusion.12
  29.2 1.9 constant_dynamic-slice_fusion.1
  31.1 147.6 %attend_forward.1 = (bf16[8,64,2048]{2,1,0:T(8,128)(2,1)}, f32[64,2048]{1,0:T(8,128)}, f32[2,2,1,256]{3,2,1,0:T(1,128)}, f32[2,2,128,256]{3,2,1,0:T(8,128)}, bf16[16,2,2,256,256]{4,3,2,1,0:T(8,128)(2,1)}) custom-call(s32[16]{0:T(128)} %compare_select_fusion.sel, bf16[2,256,256]{2,1,0:T(8,128)(2,1)} %convert_element_type.152.q, ...), custom_call_target="tpu_custom_call" | custom-call | tf_op jit(solution)/shard_map/attend_forward/pallas_call | solution.py:242
  180.3 2.2 convolution_convert_fusion.10
  182.6 1.4 fusion.83
  191.3 2.4 fusion.45
  196.4 1.8 fusion.41
  201.7 1.9 multiply_convert_fusion.1
  204.9 2.6 fusion.4
  209.6 2.0 copy.77.w_router
  215.7 3.3 fusion.7
  219.1 2.1 fusion.6
  221.2 2.0 fusion.5
  224.0 1.5 constant_dynamic-update-slice_fusion.2
  226.3 1.5 constant_dynamic-update-slice_fusion.1
  228.6 1.5 constant_dynamic-update-slice_fusion.w1
  230.1 129.6 %second_norm_backward.1 = (bf16[8,64,2048]{2,1,0:T(8,128)(2,1)}, f32[64,2048]{1,0:T(8,128)}, f32[1,2048]{1,0:T(1,128)}, f32[1,128]{1,0:T(1,128)}, bf16[2640,128]{1,0:T(8,128)(2,1)}) custom-call(bf16[8,64,2048]{2,1,0:T(8,128)(2,1)} %bitcast.159, f32[1,128]{1,0:T(1,128)} %pad.15.gate_part, f32[64,2048]{1,0:T(8,128)} %get-tuple-element.36.mixed, ...), custom_call_target="tpu_custom_call" | custom-call | tf_op jit(solution)/shard_map/second_norm_backward/pallas_call | solution.py:417
  359.7 1.9 fusion.15
  361.7 2.7 fusion.3
  364.4 169.1 %attend_backward.1 = (bf16[8,64,2048]{2,1,0:T(8,128)(2,1)}, bf16[2640,2048]{1,0:T(8,128)(2,1)}, f32[2,256,256]{2,1,0:T(8,128)}, f32[2,2,256,256]{3,2,1,0:T(8,128)}) custom-call(s32[16]{0:T(128)} %compare_select_fusion.sel, bf16[2,256,256]{2,1,0:T(8,128)(2,1)} %convert_element_type.152.q, bf16[16,2,2,256,256]{4,3,2,1,0:T(8,128)(2,1)} %get-tuple-element.32.kvall, ...), custom_call_target="tpu_custom_call" | custom-call | tf_op jit(solution)/shard_map/attend_backward/pallas_call | solution.py:586
  534.9 1.9 broadcast_multiply_fusion
  538.1 2.7 subtract_convert_fusion
  545.0 2.1 add_convert_fusion
  547.0 1.8 fusion.8
  548.9 1.9 fusion.9
  550.7 1.8 fusion.10
  552.8 3.3 fusion.11
  558.2 115.4 %first_norm_backward.1 = (bf16[8,64,2048]{2,1,0:T(8,128)(2,1)}, bf16[1088,2048]{1,0:T(8,128)(2,1)}, f32[2,2048]{1,0:T(2,128)}) custom-call(bf16[8,64,2048]{2,1,0:T(8,128)(2,1)} %bitcast.157, bf16[64,2048]{1,0:T(8,128)(2,1)} %get-tuple-element.149.tok, f32[64,2048]{1,0:T(8,128)} %get-tuple-element.42.g_mixed, f32[1,2048]{1,0:T(1,128)} %bitcast.191, ...), custom_call_target="tpu_custom_call" | custom-call | tf_op jit(solution)/shard_map/first_norm_backward/pallas_call | solution.py:682
  675.1 3.3 convert_element_type.187
  678.4 3.1 slice_bitcast_fusion.2
  681.5 1.9 copy-done.2
  683.4 2.9 copy.79
  686.3 2.9 copy.80
  689.2 1.8 copy.81
  691.0 2.9 slice.123
  693.9 1.9 slice_bitcast_fusion.5
  695.8 14.2 %convert_element_type.188 = f32[2640,2048]{1,0:T(8,128)} convert(bf16[2640,2048]{1,0:T(8,128)(2,1)} %get-tuple-element.48) | non-fusion elementwise | flops 5406720 | bytes 32440320 | tf_op jit(solution)/shard_map/convert_element_type | solution.py:870
  710.0 5.9 slice_bitcast_fusion
  716.0 1.9 slice.127
  717.9 5.3 fusion.75
  (182 shorter events, 44.7 us)
Async XLA Ops:
  0.6 193.1 %copy-start = (bf16[3,2048,176]{1,2,0:T(8,128)(2,1)S(1)}, bf16[3,2048,176]{1,2,0:T(8,128)(2,1)}, u32[]{:S(2)}) copy-start(bf16[3,2048,176]{1,2,0:T(8,128)(2,1)} %param.30) | copy-start | bytes 6488068
  6.0 18.8 %copy-start.50 = (f32[512]{0:T(512)}, f32[512]{0:T(512)S(1)}, u32[]{:S(2)}) copy-start(f32[512]{0:T(512)S(1)} %add_rsqrt_fusion) | copy-start | bytes 6148
  8.8 3.7 copy-start.48
  12.5 7.6 %copy-start.16 = (f32[512,64]{1,0:T(8,128)}, f32[512,64]{1,0:T(8,128)S(1)}, u32[]{:S(2)}) copy-start(f32[512,64]{1,0:T(8,128)S(1)} %get-tuple-element.143) | copy-start | bytes 393220
  24.8 2.7 copy-start.26
  24.8 2.7 copy-start.27
  28.4 150.3 %copy-start.47 = (s32[512,6]{0,1:T(8,128)S(1)}, s32[512,6]{0,1:T(8,128)}, u32[]{:S(2)}) copy-start(s32[512,6]{0,1:T(8,128)} %param.32) | copy-start | bytes 36868
  180.3 2.3 copy-start.5
  180.3 3.7 copy-start.10
  182.6 1.9 copy-start.3
  182.6 1.9 copy-start.30
  187.3 3.7 copy-start.45
  187.3 6.4 copy-start.38
  191.2 3.3 copy-start.43
  193.7 1.6 copy-start.6
  194.6 1.8 copy-start.34
  194.6 1.8 copy-start.36
  194.6 13.0 %copy-start.32 = (bf16[3,32,176]{2,1,0:T(8,128)(2,1)}, bf16[3,32,176]{2,1,0:T(8,128)(2,1)S(1)}, u32[]{:S(2)}) copy-start(bf16[3,32,176]{2,1,0:T(8,128)(2,1)S(1)} %get-tuple-element.136) | copy-start | bytes 101380
  196.4 1.9 copy-start.4
  196.4 2.0 copy-start.22
  198.4 1.6 copy-start.11
  198.4 2.0 copy-start.23
  204.9 2.6 copy-start.7
  215.7 3.3 copy-start.42
  219.1 2.1 copy-start.12
  219.1 2.1 copy-start.39
  221.2 2.0 copy-start.35
  230.1 129.6 %copy-start.9 = (f32[3,32,2048]{2,1,0:T(8,128)S(1)}, f32[3,32,2048]{2,1,0:T(8,128)}, u32[]{:S(2)}) copy-start(f32[3,32,2048]{2,1,0:T(8,128)} %get-tuple-element.147) | copy-start | bytes 2359300
  359.7 2.0 copy-start.24
  359.7 2.0 copy-start.40
  533.5 4.6 copy-start.17
  538.1 3.5 copy-start.28
  543.1 1.8 copy-start.25
  544.9 2.1 copy-start.13
  544.9 2.1 copy-start.49
  544.9 2.1 copy-start.51
  550.7 1.8 copy-start.18
  552.6 3.6 copy-start.52
  552.6 4.0 copy-start.8
  552.6 4.0 copy-start.46
  552.8 4.1 copy-start.15
  678.4 5.0 copy-start.2
  691.0 25.0 %slice-start = ((s8[10813440]{0:T(1024)(128)(4,1)}), s8[4194304]{0:T(1024)(128)(4,1)S(1)}, s32[]{:S(2)}) async-start(s8[10813440]{0:T(1024)(128)(4,1)} %bitcast.143), calls=%async_computation | async-start | bytes 8388608
  695.8 20.2 %slice-start.1 = ((s8[10813440]{0:T(1024)(128)(4,1)}), s8[4194304]{0:T(1024)(128)(4,1)S(1)}, s32[]{:S(2)}) async-start(s8[10813440]{0:T(1024)(128)(4,1)} %bitcast.143), calls=%async_computation.1 | async-start | bytes 8388608
  695.8 20.2 %slice-start.2 = ((s8[10813440]{0:T(1024)(128)(4,1)}), s8[2424832]{0:T(1024)(128)(4,1)S(1)}, s32[]{:S(2)}) async-start(s8[10813440]{0:T(1024)(128)(4,1)} %bitcast.143), calls=%async_computation.2 | async-start | bytes 4849664
  717.9 5.3 copy-start.19
  723.3 2.3 copy-start.20
  723.3 3.7 copy-start.1
  (8 other events, 10.8 us)

commit v2 on v0

v2 whole, which is shorter than its diff:
```python
import jax
import jax.numpy as jnp
from jax import lax
from jax.experimental import pallas as pl
from jax.experimental.pallas import tpu as pltpu
from jax.sharding import PartitionSpec as P

HD = 128
CAP = 32
EPSILON = 1e-06
ROPE_BASE = 10000.0
PRECISE = lax.Precision.HIGHEST
MESH = pl.DeviceIdType.MESH
BF = jnp.bfloat16
F32 = jnp.float32
D = 2048
SH = 352
EF = 176
R1 = 3 * SH + 9 * EF
R2 = 64 + 4 * 256
VM = 60 * 2**20
NEG = -1e30


def nt(a, b):
    return lax.dot_general(a, b, (((1,), (1,)), ((), ())), preferred_element_type=F32)


def nn(a, b):
    return lax.dot_general(a, b, (((1,), (0,)), ((), ())), preferred_element_type=F32)


def tn(a, b):
    return lax.dot_general(a, b, (((0,), (0,)), ((), ())), preferred_element_type=F32)


def turned(a):
    return jnp.transpose(a.astype(F32)).astype(BF)


def place():
    c = lax.axis_index("ctx")
    return lax.div(c, 4), lax.rem(lax.div(c, 2), 2), lax.rem(c, 2), lax.axis_index("mp")


def chip_at(dy, t):
    y, z, core, m = place()
    return lax.rem(y + dy, 4) * 2 + lax.rem(z + t, 2)


def peer(dy, t):
    y, z, core, m = place()
    return {"ctx": chip_at(dy, t) * 2 + core}


def sibling():
    y, z, core, m = place()
    return {"ctx": chip_at(0, 0) * 2 + 1 - core}


def mp_at(d):
    m = lax.axis_index("mp")
    return lax.rem(lax.div(m, 2) + d // 2, 4) * 2 + lax.rem(lax.rem(m, 2) + d % 2, 2)


def remote(src, dst, ssem, rsem, dev):
    return pltpu.make_async_remote_copy(
        src_ref=src, dst_ref=dst, send_sem=ssem, recv_sem=rsem, device_id=dev, device_id_type=MESH
    )


def greet(far=False):
    bar = pltpu.get_barrier_semaphore()
    devs = [sibling(), peer(0, 1), peer(1, 0), peer(3, 0)] + ([peer(2, 0)] if far else [])
    devs += [{"mp": mp_at(d)} for d in range(1, 8)]
    for dev in devs:
        pl.semaphore_signal(bar, inc=1, device_id=dev, device_id_type=MESH)
    return len(devs)


def all_in(count):
    pl.semaphore_wait(pltpu.get_barrier_semaphore(), count)


def mp_send_parts(parts, landing, ssem, rsem):
    m = lax.axis_index("mp")
    for d in range(1, 8):
        t = mp_at(d)
        remote(parts.at[t], landing.at[m], ssem.at[d - 1], rsem.at[m], {"mp": t}).start()


def mp_send_same(src, landing, ssem, rsem):
    m = lax.axis_index("mp")
    for d in range(1, 8):
        remote(src, landing.at[m], ssem.at[d - 1], rsem.at[m], {"mp": mp_at(d)}).start()


def mp_wait_recv(landing, ssem, rsem, d):
    t = mp_at(d)
    remote(landing.at[t], landing.at[t], ssem.at[0], rsem.at[t], {"mp": t}).wait_recv()
    return t


def mp_wait_send(src, ssem):
    for d in range(1, 8):
        remote(src, src, ssem.at[d - 1], ssem.at[d - 1], {"mp": mp_at(d)}).wait_send()


class Gather:
    def __init__(self, buf, sems):
        self.buf, (self.s, self.r) = buf, sems
        y, z, self.core, m = place()

    @staticmethod
    def sems():
        return (pltpu.SemaphoreType.DMA((15,)), pltpu.SemaphoreType.DMA((16,)))

    def send(self, src, chip, n, dev):
        dst = self.buf.at[chip, self.core]
        remote(src, dst, self.s.at[n], self.r.at[chip * 2 + self.core], dev).start()

    def start(self, src):
        chip = chip_at(0, 0)
        for n, dev in enumerate([peer(0, 1), peer(1, 0), peer(3, 0), sibling()]):
            self.send(src, chip, n, dev)

    def wait(self, chip, core):
        ref = self.buf.at[chip, core]
        remote(ref, ref, self.s.at[0], self.r.at[chip * 2 + core], sibling()).wait_recv()

    def hop(self, dy, t):
        chip = chip_at(dy, t)
        self.wait(chip, self.core)
        src = self.buf.at[chip, self.core]
        n, devs = {
            (0, 1): (4, [peer(1, 0), peer(3, 0), sibling()]),
            (3, 0): (7, [peer(1, 0), sibling()]),
            (1, 0): (9, [sibling()]),
            (3, 1): (10, [sibling()]),
            (1, 1): (11, [peer(3, 0), sibling()]),
            (2, 0): (13, [sibling()]),
            (2, 1): (14, [sibling()]),
        }[dy, t]
        for i, dev in enumerate(devs):
            self.send(src, chip, n + i, dev)
        return chip

    def other_core(self, dy, t):
        chip = chip_at(dy, t)
        self.wait(chip, 1 - self.core)

    def drain(self):
        ref = self.buf.at[0, 0]
        for n in range(15):
            remote(ref, ref, self.s.at[n], self.s.at[n], sibling()).wait_send()


HOPS = ((0, 1), (3, 0), (1, 0), (3, 1), (1, 1), (2, 0), (2, 1))


def add_rows(dst, srcs, tile):
    def body(r, carry):
        rr = pl.ds(pl.multiple_of(r * tile, 16), tile)
        total = srcs[0][rr, :].astype(F32)
        for s in srcs[1:]:
            total = total + s[rr, :].astype(F32)
        dst[rr, :] = total.astype(dst.dtype)
        return carry

    lax.fori_loop(0, dst.shape[0] // tile, body, 0)


class Scatter:
    def __init__(self, refs, tile):
        (
            self.to_sib, self.from_sib, self.sums, self.half, self.pairs,
            self.s_sib, self.r_sib, self.s_half, self.r_half, self.s_pair, self.r_pair,
        ) = refs
        self.tile = tile
        self.y, self.z, self.core, m = place()

    @staticmethod
    def scratch(rows, cols):
        dma = pltpu.SemaphoreType.DMA
        eight = pltpu.VMEM((8, rows, cols), BF)
        return (
            eight, eight, eight, pltpu.VMEM((2, rows, cols), BF), pltpu.VMEM((2, 2, rows, cols), BF),
            dma((8,)), dma((8,)), dma((2,)), dma((2,)), dma((2,)), dma((2,)),
        )

    def add(self, dst, srcs):
        add_rows(dst, srcs, self.tile)

    def to_sibling(self, chip):
        remote(
            self.to_sib.at[chip], self.from_sib.at[chip], self.s_sib.at[chip], self.r_sib.at[chip], sibling()
        ).start()

    def merge(self, chip):
        got = self.from_sib.at[chip]
        remote(got, got, self.s_sib.at[0], self.r_sib.at[chip], sibling()).wait_recv()
        self.add(self.sums.at[chip], [self.sums.at[chip], got])

    def far(self):
        for t, dy in ((0, 1), (1, 3)):
            remote(
                self.sums.at[chip_at(2, t)], self.half.at[t], self.s_half.at[t], self.r_half.at[t], peer(dy, 0)
            ).start()

    def near(self, way):
        dy = 1 if way == 0 else 3
        got = self.half.at[way]
        remote(got, got, self.s_half.at[0], self.r_half.at[way], sibling()).wait_recv()
        mid = self.sums.at[chip_at(dy, way)]
        self.add(mid, [mid, got])
        both = self.sums.at[pl.ds(lax.rem(self.y + dy, 4) * 2, 2)]
        remote(both, self.pairs.at[way], self.s_pair.at[way], self.r_pair.at[way], peer(dy, 0)).start()

    def own(self, dst):
        for way in range(2):
            got = self.pairs.at[way]
            remote(got, got, self.s_pair.at[0], self.r_pair.at[way], sibling()).wait_recv()
        for t in (1, 0):
            zz = lax.rem(self.z + t, 2)
            self.add(
                dst.at[t], [self.sums.at[chip_at(0, t)], self.pairs.at[0, zz], self.pairs.at[1, zz]]
            )

    def drain(self):
        one, two = self.sums.at[0], self.pairs.at[0]
        for k in range(8):
            remote(one, one, self.s_sib.at[k], self.s_sib.at[k], sibling()).wait_send()
        for k in range(2):
            remote(one, one, self.s_half.at[k], self.s_half.at[k], sibling()).wait_send()
            remote(two, two, self.s_pair.at[k], self.s_pair.at[k], sibling()).wait_send()


def sds(shape, dtype):
    return jax.ShapeDtypeStruct(shape, dtype)


VMEM_SPEC = pl.BlockSpec(memory_space=pltpu.VMEM)
SMEM_SPEC = pl.BlockSpec(memory_space=pltpu.SMEM)
ANY_SPEC = pl.BlockSpec(memory_space=pl.ANY)
DMA = pltpu.SemaphoreType.DMA
MP_SEMS = (DMA((7,)), DMA((8,)))
PARTS = pltpu.VMEM((8, 64, D), BF)


def params(cid):
    return pltpu.CompilerParams(collective_id=cid, has_side_effects=True, vmem_limit_bytes=VM)


def rolled(x):
    return pltpu.roll(x, 64, axis=1)


def k1_kernel(
    sel, tokens, wq, wk, wv, wo, cosf, sinf, gain_a, gain_m,
    moe, mixed, lse, ot, q, kvall, normed, att,
    tok, w3, wov, st_m, st_l, st_a, parts, land, s_in, g_sems, mp1, mp2,
):
    y, z, core, m = place()
    chip = chip_at(0, 0)
    loads = [
        pltpu.make_async_copy(a, b, s_in.at[i])
        for i, (a, b) in enumerate(
            [(tokens, tok), (wk, w3.at[0]), (wv, w3.at[1]), (wq, w3.at[2]), (wo, wov)]
        )
    ]
    for cp in loads:
        cp.start()
    count = greet()
    loads[0].wait()

    def norm_rows(i, carry):
        rr = pl.ds(pl.multiple_of(i * 128, 128), 128)
        x = tok[rr, :].astype(F32)
        n = lax.rsqrt(jnp.mean(x * x, axis=-1, keepdims=True) + EPSILON)
        normed[rr, :] = (x * n * gain_a[...]).astype(BF)
        return carry

    lax.fori_loop(0, 4, norm_rows, 0)
    own = kvall.at[chip, core]

    def turn(lin, rr, h):
        x = lin[:, h * HD : h * HD + HD]
        return x * cosf[rr, :] + rolled(x) * sinf[rr, :]

    loads[1].wait()
    loads[2].wait()

    def keys_values(n, carry):
        rr = pl.ds(pl.multiple_of(n * 256, 256), 256)
        lin = nn(normed[rr, :], w3[0])
        for h in range(2):
            own[0, n, :, pl.ds(h * HD, HD)] = turn(lin, rr, h).astype(BF)
        own[1, n] = nn(normed[rr, :], w3[1]).astype(BF)
        return carry

    lax.fori_loop(0, 2, keys_values, 0)
    all_in(count)
    gather = Gather(kvall, g_sems)
    gather.start(own)
    loads[3].wait()

    def queries(n, carry):
        rr = pl.ds(pl.multiple_of(n * 256, 256), 256)
        lin = nn(normed[rr, :], w3[2])
        for h in range(2):
            q[n, :, pl.ds(h * HD, HD)] = (turn(lin, rr, h) * (HD**-0.5)).astype(BF)
        return carry

    lax.fori_loop(0, 2, queries, 0)

    st_m[...] = jnp.full_like(st_m, NEG)
    st_l[...] = jnp.zeros_like(st_l)
    st_a[...] = jnp.zeros_like(st_a)

    def online(olds, sts, vs):
        mn = [jnp.maximum(o[0], jnp.max(s, axis=0, keepdims=True)) for o, s in zip(olds, sts)]
        ps = [jnp.exp(s - a) for s, a in zip(sts, mn)]
        al = [jnp.exp(o[0] - a) for o, a in zip(olds, mn)]
        ls = [a * o[1] + jnp.sum(p, axis=0, keepdims=True) for a, o, p in zip(al, olds, ps)]
        ac = [a * o[2] + tn(v, p.astype(BF)) for a, o, v, p in zip(al, olds, vs, ps)]
        return list(zip(mn, ls, ac))

    def keep(n, h, new):
        st_m[n, h], st_l[n, h], st_a[n, h] = new

    def block(k, cr):
        s = sel[k * 2 + cr]
        sts, vs, olds = [], [], []
        for h in range(2):
            cols = pl.ds(h * HD, HD)
            k0, k1 = kvall[k, cr, 0, 0, :, cols], kvall[k, cr, 0, 1, :, cols]
            v0, v1 = kvall[k, cr, 1, 0, :, cols], kvall[k, cr, 1, 1, :, cols]
            sts += [nt(k0, q[1, :, cols]), nt(jnp.where(s == 0, k0, k1), q[s, :, cols])]
            vs += [v0, jnp.where(s == 0, v0, v1)]
            olds.append((st_m[2, h], st_l[2, h], st_a[2, h]))
            olds.append(
                (
                    jnp.where(s == 0, st_m[0, h], st_m[1, h]),
                    jnp.where(s == 0, st_l[0, h], st_l[1, h]),
                    st_a[s, h],
                )
            )
        new = online(olds, sts, vs)
        for h in range(2):
            keep(2, h, new[2 * h])
            b = new[2 * h + 1]
            for n in range(2):
                st_m[n, h] = jnp.where(s == n, b[0], st_m[n, h])
                st_l[n, h] = jnp.where(s == n, b[1], st_l[n, h])
                st_a[n, h] = jnp.where(s == n, b[2], st_a[n, h])

    tri = lax.broadcasted_iota(jnp.int32, (256, 256), 0) <= lax.broadcasted_iota(
        jnp.int32, (256, 256), 1
    )
    for h in range(2):
        cols = pl.ds(h * HD, HD)
        names = [2, 0, 1]
        sts = [nt(own[0, 0, :, cols], q[1, :, cols])]
        sts += [jnp.where(tri, nt(own[0, n, :, cols], q[n, :, cols]), NEG) for n in range(2)]
        vs = [own[1, 0, :, cols], own[1, 0, :, cols], own[1, 1, :, cols]]
        olds = [(st_m[n, h], st_l[n, h], st_a[n, h]) for n in names]
        for n, new in zip(names, online(olds, sts, vs)):
            keep(n, h, new)

    gather.wait(chip, 1 - core)
    block(chip, 1 - core)
    for dy, t in HOPS:
        k = gather.hop(dy, t)

        def cores(i, carry):
            cr = lax.rem(core + i, 2)

            @pl.when(i == 1)
            def _():
                gather.wait(k, cr)

            block(k, cr)
            return carry

        lax.fori_loop(0, 2, cores, 0)

    for h in range(2):
        for n in range(2):
            m0, l0, a0 = st_m[n, h], st_l[n, h], st_a[n, h]
            if n == 1:
                m2, l2, a2 = st_m[2, h], st_l[2, h], st_a[2, h]
                mn = jnp.maximum(m0, m2)
                e0, e2 = jnp.exp(m0 - mn), jnp.exp(m2 - mn)
                m0, l0, a0 = mn, e0 * l0 + e2 * l2, e0 * a0 + e2 * a2
            lse[n, h] = m0 + jnp.log(l0)
            o = a0 / l0
            ot[n, h] = o
            att[pl.ds(n * 256, 256), pl.ds(h * HD, HD)] = jnp.transpose(o).astype(BF)

    loads[4].wait()

    def out_cols(i, carry):
        cols = pl.ds(pl.multiple_of(i * 256, 256), 256)
        parts[:, :, cols] = nn(att[...], wov[:, cols]).reshape(8, 64, 256).astype(BF)
        return carry

    lax.fori_loop(0, 8, out_cols, 0)
    mp_send_parts(parts, land, *mp1)
    total = tok[pl.ds(pl.multiple_of(m * 64, 64), 64), :].astype(F32) + parts[m].astype(F32)
    for d in range(1, 8):
        total = total + land[mp_wait_recv(land, *mp1, d)].astype(F32)
    mixed[...] = total
    n = lax.rsqrt(jnp.mean(total * total, axis=-1, keepdims=True) + EPSILON)
    moe[m] = (total * n * gain_m[...]).astype(BF)
    mp_send_same(moe.at[m], moe, *mp2)

    gather.drain()
    mp_wait_send(parts.at[0], mp1[0])
    for d in range(1, 8):
        mp_wait_recv(moe, *mp2, d)
    mp_wait_send(moe.at[0], mp2[0])


def attention_forward(sel, tokens, wq, wk, wv, wo, cosf, sinf, gain_a, gain_m):
    return pl.pallas_call(
        k1_kernel,
        name="attend_forward",
        out_shape=(
            sds((8, 64, D), BF),
            sds((64, D), F32),
            sds((2, 2, 1, 256), F32),
            sds((2, 2, HD, 256), F32),
            sds((2, 256, 256), BF),
            sds((8, 2, 2, 2, 256, 256), BF),
            sds((512, D), BF),
            sds((512, 256), BF),
        ),
        in_specs=[SMEM_SPEC] + [ANY_SPEC] * 5 + [VMEM_SPEC] * 4,
        out_specs=(VMEM_SPEC,) * 8,
        scratch_shapes=[
            pltpu.VMEM((512, D), BF),
            pltpu.VMEM((3, D, 256), BF),
            pltpu.VMEM((256, D), BF),
            pltpu.VMEM((3, 2, 1, 256), F32),
            pltpu.VMEM((3, 2, 1, 256), F32),
            pltpu.VMEM((3, 2, HD, 256), F32),
            PARTS, PARTS, DMA((5,)), Gather.sems(), MP_SEMS, MP_SEMS,
        ],
        compiler_params=params(1),
    )(sel, tokens, wq, wk, wv, wo, cosf, sinf, gain_a, gain_m)


def swish_parts(g, u):
    s = 1.0 / (1.0 + jnp.exp(-g))
    return s, g * s


def to_column(row):
    return jnp.transpose(jnp.broadcast_to(row, (HD, HD)))[:, 0:1]


def to_row(col):
    return jnp.transpose(jnp.broadcast_to(col, (HD, HD)))[0:1, :]


def k2_kernel(
    ids, moe, mixed, gain, w_router, cot, sg, su, sd, eg, eu, ed,
    g_attn, g_mixed, gain_part, wown, moe_part, g_logits,
    wsg, wsu, wsd, weg, weu, wed, cotv, tb, tbt, pr, gt, ut, hs, gsg, gsu,
    ein, gsl, geo, gated, eo, gein, ge3, ue3, he3, tmp, amat, blk, gate_part, gmi, land, gate_land,
    s_in, rs_refs, mp1, mp2, mp3,
):
    y, z, core, m = place()
    loads = [
        pltpu.make_async_copy(a, b, s_in.at[i])
        for i, (a, b) in enumerate(
            [(sg, wsg), (su, wsu), (eg, weg), (eu, weu), (ed, wed), (sd, wsd), (cot, cotv)]
        )
    ]
    for cp in loads:
        cp.start()
    count = greet()

    slot = lax.broadcasted_iota(jnp.int32, (HD, 512), 0)
    holder = lax.div(slot, CAP)
    chosen = holder == ids[0:1, :]
    for k in range(1, 6):
        chosen = chosen | (holder == ids[k : k + 1, :])
    chosen = jnp.where(chosen & (slot < 3 * CAP), 1.0, 0.0)
    upto = lax.broadcasted_iota(jnp.int32, (512, 512), 0) <= lax.broadcasted_iota(
        jnp.int32, (512, 512), 1
    )
    place_of = nn(chosen.astype(BF), jnp.where(upto, 1.0, 0.0).astype(BF)) - 1.0
    table_t = jnp.where(place_of == lax.rem(slot, CAP).astype(F32), chosen, 0.0)
    tbt[...] = table_t.astype(BF)
    table = jnp.transpose(table_t)
    tb[...] = table.astype(BF)
    expert = lax.div(lax.broadcasted_iota(jnp.int32, (512, HD), 1), CAP)

    logits = nt(moe[...], w_router[...])
    e = jnp.exp(logits - jnp.max(logits, axis=-1, keepdims=True))
    probs = e / jnp.sum(e, axis=-1, keepdims=True)
    pr[...] = probs
    px = jnp.where(expert == 0, probs[:, 0:1], jnp.where(expert == 1, probs[:, 1:2], probs[:, 2:3]))
    gate_col = to_column(jnp.sum(table * px, axis=0, keepdims=True))

    hs[...] = jnp.zeros_like(hs)
    gsg[...] = jnp.zeros_like(gsg)
    gsu[...] = jnp.zeros_like(gsu)
    eo[...] = jnp.zeros_like(eo)
    gein[...] = jnp.zeros_like(gein)
    tmp[...] = jnp.zeros_like(tmp)

    def gather_in(i, carry):
        cols = pl.ds(pl.multiple_of(i * 512, 512), 512)
        ein[:, cols] = nn(tbt[...], moe[:, cols]).astype(BF)
        return carry

    lax.fori_loop(0, 4, gather_in, 0)
    loads[0].wait()
    loads[1].wait()

    def shared_in(i, carry):
        rr = pl.ds(pl.multiple_of(i * 256, 256), 256)
        g, u = nt(moe[rr, :], wsg[...]), nt(moe[rr, :], wsu[...])
        gt[rr, :] = g
        ut[rr, :] = u
        hs[rr, 0:SH] = (swish_parts(g, u)[1] * u).astype(BF)
        return carry

    lax.fori_loop(0, 2, shared_in, 0)
    for cp in loads[2:5]:
        cp.wait()
    for k in range(3):
        rr = pl.ds(k * CAP, CAP)
        g, u = nt(ein[rr, :], weg[k]), nt(ein[rr, :], weu[k])
        ge3[k] = g
        ue3[k] = u
        hid = (swish_parts(g, u)[1] * u).astype(BF)
        he3[k] = hid
        eo[rr, :] = nn(hid, wed[k])
    loads[5].wait()
    loads[6].wait()

    def slots_in(i, carry):
        cols = pl.ds(pl.multiple_of(i * 512, 512), 512)
        g = nn(tbt[...], cotv[:, cols])
        gsl[:, cols] = g.astype(BF)
        geo[:, cols] = (gate_col * g).astype(BF)
        gated[:, cols] = (gate_col * eo[:, cols]).astype(BF)
        return carry

    lax.fori_loop(0, 4, slots_in, 0)
    gate_part[...] = to_row(jnp.sum(eo[...] * gsl[...].astype(F32), axis=1, keepdims=True))
    all_in(count)
    mp_send_same(gate_part, gate_land, *mp1)

    def shared_back(i, carry):
        rr = pl.ds(pl.multiple_of(i * 256, 256), 256)
        gh = nt(cotv[rr, :], wsd[...])
        g, u = gt[rr, :], ut[rr, :]
        s, sw = swish_parts(g, u)
        gsg[rr, 0:SH] = (gh * u * s * (1.0 + g * (1.0 - s))).astype(BF)
        gsu[rr, 0:SH] = (gh * sw).astype(BF)
        return carry

    lax.fori_loop(0, 2, shared_back, 0)

    def put_block(i, k, val):
        rr = pl.ds(k * CAP, CAP)
        tmp[k, rr, 0:EF] = val.astype(F32)
        blk[pl.ds(EF * i, EF), :] = jnp.transpose(tmp[k])[0:EF].astype(BF)

    for k in range(3):
        rr = pl.ds(k * CAP, CAP)
        gh = nt(geo[rr, :], wed[k])
        g, u = ge3[k], ue3[k]
        s, sw = swish_parts(g, u)
        geg = (gh * u * s * (1.0 + g * (1.0 - s))).astype(BF)
        geu = (gh * sw).astype(BF)
        gein[rr, :] = (nn(geg, weg[k]) + nn(geu, weu[k])).astype(BF)
        put_block(k, k, geg)
        put_block(3 + k, k, geu)
        put_block(6 + k, k, he3[k])

    def back_cols(i, carry):
        cols = pl.ds(pl.multiple_of(i * 256, 256), 256)
        g = nn(gsg[:, 0:SH], wsg[:, cols]) + nn(gsu[:, 0:SH], wsu[:, cols]) + nn(tb[...], gein[:, cols])
        gmi[:, :, cols] = g.reshape(8, 64, 256).astype(BF)
        return carry

    lax.fori_loop(0, 8, back_cols, 0)
    mp_send_parts(gmi, land, *mp2)

    amat[pl.ds(0, SH), :] = turned(gsg[...])[0:SH]
    amat[pl.ds(SH, SH), :] = turned(gsu[...])[0:SH]
    amat[pl.ds(2 * SH, SH), :] = turned(hs[...])[0:SH]
    rs = Scatter(rs_refs, 528)

    def piece(k):
        cols = pl.ds(pl.multiple_of(k * 256, 256), 256)
        for off, rows, lhs, rhs in (
            (0, 2 * SH, amat.at[pl.ds(0, 2 * SH)], moe),
            (2 * SH, SH, amat.at[pl.ds(2 * SH, SH)], cotv),
            (3 * SH, 6 * EF, blk.at[pl.ds(0, 6 * EF)], ein),
            (3 * SH + 6 * EF, 3 * EF, blk.at[pl.ds(6 * EF, 3 * EF)], geo),
        ):
            val = nn(lhs[...], rhs[:, cols]).astype(BF)
            one, two = val[:, 0:HD], val[:, HD:]
            rs.sums[k, pl.ds(off, rows), :] = jnp.where(core == 0, one, two)
            rs.to_sib[k, pl.ds(off, rows), :] = jnp.where(core == 0, two, one)
        rs.to_sibling(k)

    def pieces(i, carry):
        j = lax.div(i, 2)
        dy = lax.rem(2 - j + 3 * lax.div(j * (j - 1), 2), 4)
        piece(chip_at(dy, lax.rem(i, 2)))

        @pl.when(i == 2)
        def _():
            rs.merge(chip_at(2, 0))
            rs.merge(chip_at(2, 1))
            rs.far()

        return carry

    lax.fori_loop(0, 8, pieces, 0)

    def out_cols(i, carry):
        cols = pl.ds(pl.multiple_of(i * 256, 256), 256)
        o = nn(hs[:, 0:SH], wsd[:, cols]) + nn(tb[...], gated[:, cols])
        moe_part[:, :, cols] = o.reshape(8, 64, 256).astype(BF)
        return carry

    lax.fori_loop(0, 8, out_cols, 0)

    gate = gate_part[...]
    for d in range(1, 8):
        gate = gate + gate_land[mp_wait_recv(gate_land, *mp1, d)]
    lane2 = lax.broadcasted_iota(jnp.int32, (HD, 64), 0)
    col2 = lax.broadcasted_iota(jnp.int32, (HD, 64), 1)
    member = jnp.where((lax.div(lane2, CAP) == col2) & (col2 < 3), 1.0, 0.0)
    gate_probs = lax.dot_general(
        tb[...].astype(F32) * gate, member, (((1,), (0,)), ((), ())),
        precision=PRECISE, preferred_element_type=F32,
    )
    prob = pr[...]
    g_logits[...] = (prob * (gate_probs - jnp.sum(gate_probs * prob, axis=-1, keepdims=True))).astype(BF)

    for way, dy in ((0, 1), (1, 3)):
        rs.merge(chip_at(dy, 0))
        rs.merge(chip_at(dy, 1))
        rs.near(way)
    rs.merge(chip_at(0, 1))
    rs.merge(chip_at(0, 0))

    mine = pl.ds(pl.multiple_of(m * 64, 64), 64)
    total = nn(g_logits[mine, :], w_router[...]) + gmi[m].astype(F32)
    for d in range(1, 8):
        total = total + land[mp_wait_recv(land, *mp2, d)].astype(F32)
    mx = mixed[...]
    n = lax.rsqrt(jnp.mean(mx * mx, axis=-1, keepdims=True) + EPSILON)
    gain_part[...] = jnp.sum(total * mx * n, axis=0, keepdims=True)
    gg = total * gain[...]
    gm = cotv[mine, :].astype(F32) + n * gg
    gm = gm - mx * (n * n * n) * jnp.mean(gg * mx, axis=-1, keepdims=True)
    g_mixed[...] = gm
    g_attn[m] = gm.astype(BF)
    mp_send_same(g_attn.at[m], g_attn, *mp3)

    rs.own(wown)
    rs.drain()
    mp_wait_send(gmi.at[0], mp2[0])
    mp_wait_send(gate_part, mp1[0])
    for d in range(1, 8):
        mp_wait_recv(g_attn, *mp3, d)
    mp_wait_send(g_attn.at[0], mp3[0])


def experts(ids, moe, mixed, gain, w_router, cot, sg, su, sd, eg, eu, ed):
    vm = pltpu.VMEM
    return pl.pallas_call(
        k2_kernel,
        name="experts",
        out_shape=(
            sds((8, 64, D), BF),
            sds((64, D), F32),
            sds((1, D), F32),
            sds((2, R1, HD), BF),
            sds((8, 64, D), BF),
            sds((512, 64), BF),
        ),
        in_specs=[VMEM_SPEC] * 5 + [ANY_SPEC] * 7,
        out_specs=(VMEM_SPEC,) * 6,
        scratch_shapes=[
            vm((SH, D), BF), vm((SH, D), BF), vm((SH, D), BF),
            vm((3, EF, D), BF), vm((3, EF, D), BF), vm((3, EF, D), BF),
            vm((512, D), BF), vm((512, HD), BF), vm((HD, 512), BF), vm((512, 64), F32),
            vm((512, SH), F32), vm((512, SH), F32),
            vm((512, 384), BF), vm((512, 384), BF), vm((512, 384), BF),
            vm((HD, D), BF), vm((HD, D), BF), vm((HD, D), BF), vm((HD, D), BF),
            vm((HD, D), F32), vm((HD, D), BF),
            vm((3, CAP, EF), F32), vm((3, CAP, EF), F32), vm((3, CAP, EF), BF),
            vm((3, HD, 256), F32), vm((3 * SH, 512), BF), vm((9 * EF, HD), BF),
            vm((1, HD), F32), PARTS, PARTS, vm((8, 1, HD), F32),
            DMA((7,)), Scatter.scratch(R1, HD), MP_SEMS, MP_SEMS, MP_SEMS,
        ],
        compiler_params=params(2),
    )(ids, moe, mixed, gain, w_router, cot, sg, su, sd, eg, eu, ed)


def k3_kernel(
    sel, q, kvall, lse, ot, g_attn, wout, moe_part, mixed, wown, cosf, sinf,
    output, w1, glin,
    do, delta, dqt, oland, zbuf, fin, dkz, dkv,
    s_loc, s_z, r_z, s_z2, r_z2, g_sems, rs_refs, mp1, mp2,
):
    y, z, core, m = place()
    chip = chip_at(0, 0)
    count = greet()
    g_att = nt(g_attn[...], wout[...])
    for n in range(2):
        for h in range(2):
            piece = g_att[n * 256 : n * 256 + 256, h * HD : h * HD + HD].astype(BF)
            do[n, h] = piece
            delta[n, h] = jnp.sum(jnp.transpose(piece.astype(F32)) * ot[n, h], axis=0, keepdims=True)
    dqt[...] = jnp.zeros_like(dqt)
    all_in(count)
    mp_send_parts(moe_part, oland, *mp1)
    remote(wown.at[1], zbuf, s_z, r_z, peer(0, 1)).start()
    rs = Scatter(rs_refs, 256)
    gather = Gather(w1, g_sems)

    def terms(items):
        ps = [nt(k, qq) - ls for k, v, qq, dd, ls, de, mask in items]
        ps = [jnp.exp(p) for p in ps]
        ps = [p if i[6] is None else jnp.where(i[6], p, 0.0) for p, i in zip(ps, items)]
        ds = [(p * (nt(i[1], i[3]) - i[5])).astype(BF) for p, i in zip(ps, items)]
        dv = [nn(p.astype(BF), i[3]) for p, i in zip(ps, items)]
        dk = [nn(d, i[2]) for d, i in zip(ds, items)]
        dq = [tn(i[0], d) for d, i in zip(ds, items)]
        return list(zip(dk, dv, dq))

    def block(k, cr, dst):
        s = sel[k * 2 + cr]
        items = []
        for h in range(2):
            cols = pl.ds(h * HD, HD)
            items.append(
                (kvall[k, cr, 0, 0, :, cols], kvall[k, cr, 1, 0, :, cols], q[1, :, cols], do[1, h],
                 lse[1, h], delta[1, h], None)
            )
            items.append(
                (kvall[k, cr, 0, s, :, cols], kvall[k, cr, 1, s, :, cols], q[s, :, cols], do[s, h],
                 jnp.where(s == 0, lse[0, h], lse[1, h]), jnp.where(s == 0, delta[0, h], delta[1, h]), None)
            )
        got = terms(items)
        for h in range(2):
            cols = pl.ds(h * HD, HD)
            always, picked = got[2 * h], got[2 * h + 1]
            dqt[2, h] += always[2]
            for n in range(2):
                dqt[n, h] += jnp.where(s == n, picked[2], 0.0)
            for a in range(2):
                low = always[a] + jnp.where(s == 0, picked[a], 0.0)
                high = jnp.where(s == 1, picked[a], 0.0)
                dst[pl.ds(a * 512, 256), cols] = low.astype(BF)
                dst[pl.ds(a * 512 + 256, 256), cols] = high.astype(BF)

    def both_cores(k):
        block(k, 1 - core, rs.to_sib.at[k])
        rs.to_sibling(k)
        block(k, core, rs.sums.at[k])

    def ring_place(dy):
        def one(t, carry):
            both_cores(chip_at(dy, t))
            return carry

        lax.fori_loop(0, 2, one, 0)
        rs.merge(chip_at(dy, 0))
        rs.merge(chip_at(dy, 1))

    ring_place(2)
    rs.far()
    ring_place(1)
    rs.near(0)
    ring_place(3)
    rs.near(1)

    remote(zbuf, zbuf, s_z, r_z, peer(0, 1)).wait_recv()
    add_rows(fin, [wown.at[0], zbuf], 528)
    gather.start(fin)
    local = pltpu.make_async_copy(fin, w1.at[chip, core], s_loc)
    local.start()

    both_cores(chip_at(0, 1))
    block(chip, 1 - core, rs.to_sib.at[chip])
    rs.to_sibling(chip)
    tri = lax.broadcasted_iota(jnp.int32, (256, 256), 0) <= lax.broadcasted_iota(
        jnp.int32, (256, 256), 1
    )
    for h in range(2):
        cols = pl.ds(h * HD, HD)
        kk = [kvall[chip, core, 0, n, :, cols] for n in range(2)]
        vv = [kvall[chip, core, 1, n, :, cols] for n in range(2)]
        items = [(kk[0], vv[0], q[1, :, cols], do[1, h], lse[1, h], delta[1, h], None)]
        for n in range(2):
            items.append((kk[n], vv[n], q[n, :, cols], do[n, h], lse[n, h], delta[n, h], tri))
        got = terms(items)
        dqt[2, h] += got[0][2]
        for n in range(2):
            dqt[n, h] += got[1 + n][2]
        for a in range(2):
            rs.sums[chip, pl.ds(a * 512, 256), cols] = (got[0][a] + got[1][a]).astype(BF)
            rs.sums[chip, pl.ds(a * 512 + 256, 256), cols] = got[2][a].astype(BF)
    rs.merge(chip_at(0, 1))
    rs.merge(chip)

    def back(x, rr):
        return (x * cosf[rr, :] - rolled(x) * sinf[rr, :]).astype(BF)

    for h in range(2):
        for n in range(2):
            rr = pl.ds(n * 256, 256)
            g = dqt[n, h] if n == 0 else dqt[1, h] + dqt[2, h]
            glin[0, rr, pl.ds(h * HD, HD)] = back(jnp.transpose(g) * (HD**-0.5), rr)

    total = mixed[...] + moe_part[m].astype(F32)
    for d in range(1, 8):
        total = total + oland[mp_wait_recv(oland, *mp1, d)].astype(F32)
    output[m] = total.astype(BF)
    mp_send_same(output.at[m], output, *mp2)

    gather.hop(0, 1)
    gather.hop(3, 0)
    gather.hop(1, 0)
    rs.own(dkz)
    remote(dkz.at[1], dkv, s_z2, r_z2, peer(0, 1)).start()
    remote(dkv, dkv, s_z2, r_z2, peer(0, 1)).wait_recv()
    for n in range(2):
        rr = pl.ds(n * 256, 256)
        for h in range(2):
            cols = pl.ds(h * HD, HD)
            kr = pl.ds(n * 256, 256)
            vr = pl.ds(512 + n * 256, 256)
            g = dkz[0, kr, cols].astype(F32) + dkv[kr, cols].astype(F32)
            glin[1, rr, cols] = back(g, rr)
            glin[2, rr, cols] = (dkz[0, vr, cols].astype(F32) + dkv[vr, cols].astype(F32)).astype(BF)
    for dy, t in HOPS[3:]:
        gather.hop(dy, t)

    remote(dkv, dkv, s_z2, s_z2, peer(0, 1)).wait_send()
    remote(zbuf, zbuf, s_z, s_z, peer(0, 1)).wait_send()
    rs.drain()
    mp_wait_send(moe_part.at[0], mp1[0])
    for d in range(1, 8):
        mp_wait_recv(output, *mp2, d)
    mp_wait_send(output.at[0], mp2[0])
    local.wait()
    gather.wait(chip, 1 - core)
    for dy, t in HOPS:
        gather.other_core(dy, t)
    gather.drain()


def attention_backward(sel, q, kvall, lse, ot, g_attn, wout, moe_part, mixed, wown, cosf, sinf):
    vm = pltpu.VMEM
    return pl.pallas_call(
        k3_kernel,
        name="attend_backward",
        out_shape=(sds((8, 64, D), BF), sds((8, 2, R1, HD), BF), sds((3, 512, 256), BF)),
        in_specs=[SMEM_SPEC] + [VMEM_SPEC] * 11,
        out_specs=(VMEM_SPEC, ANY_SPEC, VMEM_SPEC),
        scratch_shapes=[
            vm((2, 2, 256, HD), BF), vm((2, 2, 1, 256), F32), vm((3, 2, HD, 256), F32),
            PARTS, vm((R1, HD), BF), vm((R1, HD), BF), vm((2, 1024, 256), BF), vm((1024, 256), BF),
            DMA, DMA, DMA, DMA, DMA, Gather.sems(), Scatter.scratch(1024, 256), MP_SEMS, MP_SEMS,
        ],
        compiler_params=params(3),
    )(sel, q, kvall, lse, ot, g_attn, wout, moe_part, mixed, wown, cosf, sinf)


def k4_kernel(
    glin, att, g_attn, g_logits, moe, normed, g_mixed, gain, gain_moe_part, tokens, wq, wk, wv,
    g_tokens, w2out, gains,
    tok, w3, amat, gni, land, zbuf, fin, wown, gmine, gland, gsteps, gfar,
    s_in, s_loc, s_z, r_z, s_gx, r_gx, s_gy, r_gy, g_sems, rs_refs, mp1, mp2, mp3,
):
    y, z, core, m = place()
    chip = chip_at(0, 0)
    loads = [
        pltpu.make_async_copy(a, w3.at[i], s_in.at[i]) for i, a in enumerate((wq, wk, wv))
    ]
    mine = pl.ds(pl.multiple_of(m * 64, 64), 64)
    loads.append(pltpu.make_async_copy(tokens.at[mine, :], tok, s_in.at[3]))
    for cp in loads:
        cp.start()
    count = greet(far=True)
    for cp in loads:
        cp.wait()

    def back_cols(i, carry):
        cols = pl.ds(pl.multiple_of(i * 256, 256), 256)
        g = nt(glin[0], w3[0, cols, :]) + nt(glin[1], w3[1, cols, :]) + nt(glin[2], w3[2, cols, :])
        gni[:, :, cols] = g.reshape(8, 64, 256).astype(BF)
        return carry

    lax.fori_loop(0, 8, back_cols, 0)
    all_in(count)
    mp_send_parts(gni, land, *mp1)

    amat[pl.ds(0, 64), :] = turned(g_logits[...])
    for i in range(3):
        amat[pl.ds(64 + 256 * i, 256), :] = turned(glin[i])
    amat[pl.ds(832, 256), :] = turned(att[...])
    rs = Scatter(rs_refs, 544)

    def piece(k):
        cols = pl.ds(pl.multiple_of(k * 256, 256), 256)
        for off, rows, rhs in ((0, 64, moe), (64, 768, normed), (832, 256, g_attn)):
            val = nn(amat[pl.ds(off, rows), :], rhs[:, cols]).astype(BF)
            one, two = val[:, 0:HD], val[:, HD:]
            rs.sums[k, pl.ds(off, rows), :] = jnp.where(core == 0, one, two)
            rs.to_sib[k, pl.ds(off, rows), :] = jnp.where(core == 0, two, one)
        rs.to_sibling(k)

    def pieces(i, carry):
        j = lax.div(i, 2)
        dy = lax.rem(2 - j + 3 * lax.div(j * (j - 1), 2), 4)
        piece(chip_at(dy, lax.rem(i, 2)))

        @pl.when(i == 2)
        def _():
            rs.merge(chip_at(2, 0))
            rs.merge(chip_at(2, 1))
            rs.far()

        return carry

    lax.fori_loop(0, 8, pieces, 0)
    for way, dy in ((0, 1), (1, 3)):
        rs.merge(chip_at(dy, 0))
        rs.merge(chip_at(dy, 1))
        rs.near(way)
    rs.merge(chip_at(0, 1))
    rs.merge(chip_at(0, 0))

    total = gni[m].astype(F32)
    for d in range(1, 8):
        total = total + land[mp_wait_recv(land, *mp1, d)].astype(F32)
    src = tok[...].astype(F32)
    n = lax.rsqrt(jnp.mean(src * src, axis=-1, keepdims=True) + EPSILON)
    gg = total * gain[...]
    gs = n * gg - src * (n * n * n) * jnp.mean(gg * src, axis=-1, keepdims=True)
    g_tokens[m] = (g_mixed[...] + gs).astype(BF)
    mp_send_same(g_tokens.at[m], g_tokens, *mp2)
    gmine[pl.ds(0, 1), :] = gain_moe_part[...]
    gmine[pl.ds(1, 1), :] = jnp.sum(total * src * n, axis=0, keepdims=True)
    mp_send_same(gmine, gland, *mp3)

    rs.own(wown)
    remote(wown.at[1], zbuf, s_z, r_z, peer(0, 1)).start()

    gsum = gmine[...]
    for d in range(1, 8):
        gsum = gsum + gland[mp_wait_recv(gland, *mp3, d)]
    for i, dev in enumerate((sibling(), peer(0, 1))):
        gsteps[2 * i] = gsum
        cp = remote(gsteps.at[2 * i], gsteps.at[2 * i + 1], s_gx.at[i], r_gx.at[i], dev)
        cp.start()
        cp.wait_recv()
        gsum = gsum + gsteps[2 * i + 1]
    gfar[y] = gsum
    for d in range(1, 4):
        remote(gfar.at[y], gfar.at[y], s_gy.at[d - 1], r_gy.at[y], peer(d, 0)).start()

    remote(zbuf, zbuf, s_z, r_z, peer(0, 1)).wait_recv()
    add_rows(fin, [wown.at[0], zbuf], 544)
    gather = Gather(w2out, g_sems)
    gather.start(fin)
    local = pltpu.make_async_copy(fin, w2out.at[chip, core], s_loc)
    local.start()

    for d in range(1, 4):
        yy = lax.rem(y + d, 4)
        remote(gfar.at[yy], gfar.at[yy], s_gy.at[0], r_gy.at[yy], peer(d, 0)).wait_recv()
    gains[...] = gfar[0] + gfar[1] + gfar[2] + gfar[3]

    for dy, t in HOPS:
        gather.hop(dy, t)
    for i, dev in enumerate((sibling(), peer(0, 1))):
        remote(gsteps.at[0], gsteps.at[0], s_gx.at[i], s_gx.at[i], dev).wait_send()
    for d in range(1, 4):
        remote(gfar.at[0], gfar.at[0], s_gy.at[d - 1], s_gy.at[d - 1], peer(d, 0)).wait_send()
    remote(zbuf, zbuf, s_z, s_z, peer(0, 1)).wait_send()
    rs.drain()
    mp_wait_send(gmine, mp3[0])
    mp_wait_send(gni.at[0], mp1[0])
    for d in range(1, 8):
        mp_wait_recv(g_tokens, *mp2, d)
    mp_wait_send(g_tokens.at[0], mp2[0])
    local.wait()
    gather.wait(chip, 1 - core)
    for dy, t in HOPS:
        gather.other_core(dy, t)
    gather.drain()


def first_norm_backward(*args):
    vm = pltpu.VMEM
    return pl.pallas_call(
        k4_kernel,
        name="first_norm_backward",
        out_shape=(sds((8, 64, D), BF), sds((8, 2, R2, HD), BF), sds((2, D), F32)),
        in_specs=[VMEM_SPEC] * 9 + [ANY_SPEC] * 4,
        out_specs=(VMEM_SPEC, ANY_SPEC, VMEM_SPEC),
        scratch_shapes=[
            vm((64, D), BF), vm((3, D, 256), BF), vm((R2, 512), BF), PARTS, PARTS, vm((R2, HD), BF), vm((R2, HD), BF),
            vm((2, R2, HD), BF), vm((2, D), F32), vm((8, 2, D), F32), vm((4, 2, D), F32), vm((4, 2, D), F32),
            DMA((4,)), DMA, DMA, DMA, DMA((2,)), DMA((2,)), DMA((3,)), DMA((4,)),
            Gather.sems(), Scatter.scratch(R2, HD), MP_SEMS, MP_SEMS, MP_SEMS,
        ],
        compiler_params=params(4),
    )(*args)


def widen_kernel(w1, w2, gq, gk, gv, go, gr, sg, su, sd, eg, eu, ed):
    def flip(src, off):
        return jnp.transpose(src[0, 0, pl.ds(off, 256), :].astype(F32))

    gr[...] = w2[0, 0, pl.ds(0, 64), :].astype(F32)
    gq[...] = flip(w2, 64)
    gk[...] = flip(w2, 320)
    gv[...] = flip(w2, 576)
    go[...] = w2[0, 0, pl.ds(832, 256), :].astype(F32)
    sg[...] = w1[0, 0, pl.ds(0, SH), :].astype(F32)
    su[...] = w1[0, 0, pl.ds(SH, SH), :].astype(F32)
    sd[...] = w1[0, 0, pl.ds(2 * SH, SH), :].astype(F32)
    for k in range(3):
        eg[k] = w1[0, 0, pl.ds(3 * SH + EF * k, EF), :].astype(F32)
        eu[k] = w1[0, 0, pl.ds(3 * SH + EF * (3 + k), EF), :].astype(F32)
        ed[k] = w1[0, 0, pl.ds(3 * SH + EF * (6 + k), EF), :].astype(F32)


def widen(w1, w2):
    def rows(width):
        return sds((D, width), F32), pl.BlockSpec((HD, width), lambda i: (i, 0))

    def cols(height):
        return sds((height, D), F32), pl.BlockSpec((height, HD), lambda i: (0, i))

    three = sds((3, EF, D), F32), pl.BlockSpec((3, EF, HD), lambda i: (0, 0, i))
    outs = [rows(256), rows(256), rows(256), cols(256), cols(64), cols(SH), cols(SH), cols(SH)]
    outs += [three, three, three]
    return pl.pallas_call(
        widen_kernel,
        name="widen",
        grid=(16,),
        out_shape=[o[0] for o in outs],
        in_specs=[
            pl.BlockSpec((1, 1, R1, HD), lambda i: (i // 2, i % 2, 0, 0)),
            pl.BlockSpec((1, 1, R2, HD), lambda i: (i // 2, i % 2, 0, 0)),
        ],
        out_specs=[o[1] for o in outs],
        compiler_params=pltpu.CompilerParams(vmem_limit_bytes=VM),
    )(w1, w2)


def on_device(
    tokens, cotangent, gain_attn, w_query, w_key, w_value, w_out, gain_moe, w_router,
    shared_gate, shared_up, shared_down, expert_gate, expert_up, expert_down, expert_ids, pair_order,
):
    rows = tokens.shape[0]
    member = lax.axis_index("ctx")
    pair = lax.dynamic_index_in_dim(pair_order, member, keepdims=False)
    within = jnp.arange(rows, dtype=jnp.int32)
    pos = jnp.where(within < 256, pair * 256 + within, (31 - pair) * 256 + within - 256)
    inverse = ROPE_BASE ** (-2.0 * jnp.arange(HD // 2, dtype=F32) / HD)
    phase = pos.astype(F32)[:, None] * jnp.concatenate([inverse, inverse])[None, :]
    sign = jnp.where(jnp.arange(HD) < HD // 2, -1.0, 1.0).astype(F32)
    cosf = jnp.cos(phase)
    sinf = jnp.sin(phase) * sign[None, :]
    sel = jnp.where(pair_order < pair, 0, 1).astype(jnp.int32)

    moe, mixed, lse, ot, q, kvall, normed, att = attention_forward(
        sel, tokens, w_query, w_key, w_value, w_out, cosf, sinf, gain_attn[None], gain_moe[None]
    )
    moe = moe.reshape(rows, D)
    g_attn, g_mixed, gain_moe_part, wown, moe_part, g_logits = experts(
        expert_ids.T, moe, mixed, gain_moe[None], w_router.T, cotangent, shared_gate.T, shared_up.T, shared_down,
        expert_gate.transpose(0, 2, 1), expert_up.transpose(0, 2, 1), expert_down,
    )
    g_attn = g_attn.reshape(rows, D)
    output, w1, glin = attention_backward(
        sel, q, kvall, lse, ot, g_attn, w_out, moe_part, mixed, wown, cosf, sinf
    )
    g_tokens, w2, gains = first_norm_backward(
        glin, att, g_attn, g_logits, moe, normed, g_mixed, gain_attn[None], gain_moe_part,
        tokens, w_query, w_key, w_value,
    )
    gq, gk, gv, go, gr, sg, su, sd, eg, eu, ed = widen(w1, w2)
    return (
        output.reshape(rows, D), g_tokens.reshape(rows, D), gains[1],
        gq, gk, gv, go, gains[0], gr.T, sg.T, su.T, sd, eg.transpose(0, 2, 1), eu.transpose(0, 2, 1), ed,
    )


def solution(mesh):
    in_specs = (
        P("ctx", None), P("ctx", None), P(), P(None, "mp"), P(None, "mp"), P(None, "mp"),
        P("mp", None), P(), P(), P(None, "mp"), P(None, "mp"), P("mp", None),
        P(None, None, "mp"), P(None, None, "mp"), P(None, "mp", None), P("ctx", None), P(),
    )
    out_specs = (
        P("ctx", None), P("ctx", None), P(), P(None, "mp"), P(None, "mp"), P(None, "mp"),
        P("mp", None), P(), P(), P(None, "mp"), P(None, "mp"), P("mp", None),
        P(None, None, "mp"), P(None, None, "mp"), P(None, "mp", None),
    )
    return jax.shard_map(
        on_device, mesh=mesh, in_specs=in_specs, out_specs=out_specs, check_vma=False
    )
```

time: 1180 us -> 449 us (0.38)
  waiting for transfers between devices: 809 us -> 0 us
  Pallas kernels: 0 us -> 436 us
  matrix products: 180 us -> 0 us
  other arithmetic: 102 us -> 3.71 us
  blocking collectives: 49.4 us -> 0 us
  local copies, waits for them, and re-layouts: 21.3 us -> 6.31 us
  between operations: 15 us -> 2 us
    psum x4 -> x0, waiting for transfers between devices: 687 us -> none  [the longest x1 305 us: on_device(): lax.psum(grad_w_query.astype(jnp.bfloat16), 'ctx').astype(jnp.float32)]
    pallas_call x0 -> x5, Pallas kernels: none -> 436 us  [the longest x1 120 us: attention_backward(): pl.pallas_call(k3_kernel, name='attend_backward', out_shape=(sds((8, 64,...]
    dot_general x45 -> x0, matrix products: 180 us -> none  [the longest x33 157 us: contract(): return jnp.einsum(pattern, left, right, preferred_element_type=jnp.float32)]
    reduce_scatter x2 -> x0, waiting for transfers between devices: 81.9 us -> none  [the longest x1 48.8 us: on_device(): lax.psum_scatter(value_part.reshape(v_every.shape[0], -1).astype(jnp.bflo...]
    convert_element_type x18 -> x1, other arithmetic: 61.7 us -> 0.01 us  [on_device(): pos.astype(F32)[:, None] * jnp.concatenate([inverse, inverse])[None, :]]
    psum x2 -> x0, blocking collectives: 49.4 us -> none  [the longest x1 31.1 us: on_device(): lax.psum(grad_gain_attn.astype(jnp.bfloat16), 'ctx').astype(jnp.float32)]
    all_gather x2 -> x0, waiting for transfers between devices: 39.3 us -> none  [the longest x1 32.6 us: on_device(): lax.all_gather(k_rot.reshape(row_count, -1), 'ctx', axis=0, tiled=True)]
    reduce_sum x6 -> x0, other arithmetic: 24.9 us -> none  [the longest x1 15.7 us: attend_forward(): jnp.sum(jnp.exp(scores - row_max), axis=-1, keepdims=True)]
  transfers between devices with their start and end apart: 8 -> 0, of which waited for: 8 -> 0; matrix products, arithmetic and copies ran while one was open for 11% -> 0% of each run, Pallas kernels for 0% -> 0%
where the time goes in v2:
time: 449 us; the launch traced here: 448 us
  Pallas kernels  436 us (97%)
  local copies, waits for them, and re-layouts  6.31 us (1%)
    pallas_call x1, Pallas kernels, attention_backward(): pl.pallas_call(k3_kernel, name='attend_backward', out_shape=(sds((8, 64,...  120 us
    pallas_call x1, Pallas kernels, attention_forward(): pl.pallas_call(k1_kernel, name='attend_forward', out_shape=(sds((8, 64, D...  119 us
    pallas_call x1, Pallas kernels, first_norm_backward(): pl.pallas_call(k4_kernel, name='first_norm_backward', out_shape=(sds((8,...  100 us
    pallas_call x1, Pallas kernels, experts(): pl.pallas_call(k2_kernel, name='experts', out_shape=(sds((8, 64, D), BF),...  78.5 us
    pallas_call x1, Pallas kernels, widen(): pl.pallas_call(widen_kernel, name='widen', grid=(16,), out_shape=[o[0] fo...  18.6 us

profile of v2, /device:TPU:1, one launch (start us, length us, event | category | flops | bytes accessed | tf_op | source)
XLA Modules:
  0.0 448.4 jit_solution(10806202050552493413)
XLA Ops:
  0.6 1.2 dynamic_slice.4
  3.2 1.8 compare_select_fusion.1.sel
  5.0 0.1 compare_select_fusion
  5.1 1.8 fusion
  6.9 118.7 %attend_forward.1 = (bf16[8,64,2048]{2,1,0:T(8,128)(2,1)}, f32[64,2048]{1,0:T(8,128)}, f32[2,2,1,256]{3,2,1,0:T(1,128)}, f32[2,2,128,256]{3,2,1,0:T(8,128)}, bf1...) custom-call(s32[16]{0:T(128)} %compare_select_fusion.1.sel, ...), custom_call_target="tpu_custom_call" | custom-call | tf_op jit(solution)/shard_map/attend_forward/pallas_call | solution.py:425
  125.6 78.5 %experts.1 = (bf16[8,64,2048]{2,1,0:T(8,128)(2,1)}, f32[64,2048]{1,0:T(8,128)}, f32[1,2048]{1,0:T(1,128)}, bf16[2,2640,128]{2,1,0:T(8,128)(2,1)}, bf16[8,64,2048]{2,1,0:T(8,128)(2,1)}, /*index=5*/bf16[512,64]{1,0:T(8,128)(2,1)}) custom-call(s32[6,512]{1,0:T(8,128)} %bitcast.35, bf16[512,2048]{1,0:T(8,128)(2,1)} %bitcast.20, ...), custom_call_target="tpu_custom_call" | custom-call | tf_op jit(solution)/shard_map/experts/pallas_call | solution.py:682
  204.2 120.4 %attend_backward.1 = (bf16[8,64,2048]{2,1,0:T(8,128)(2,1)}, bf16[8,2,2640,128]{3,2,1,0:T(8,128)(2,1)}, bf16[3,512,256]{2,1,0:T(8,128)(2,1)}) custom-call(s32[16]{0:T(128)} %compare_select_fusion.1.sel, bf16[2,256,256]{2,1,0:T(8,128)(2,1)} %get-tuple-element.46.q, bf16[8,2,2,2,256,256]{5,4,3,2,1,0:T(8,128)(2,1)} %get-tuple-element.47.kvall, ...), custom_call_target="tpu_custom_call" | custom-call | tf_op jit(solution)/shard_map/attend_backward/pallas_call | solution.py:869
  324.6 100.1 %first_norm_backward.1 = (bf16[8,64,2048]{2,1,0:T(8,128)(2,1)}, bf16[8,2,1088,128]{3,2,1,0:T(8,128)(2,1)}, f32[2,2048]{1,0:T(2,128)}) custom-call(bf16[3,512,256]{2,1,0:T(8,128)(2,1)} %get-tuple-element.56.glin, bf16[512,256]{1,0:T(8,128)(2,1)} %get-tuple-element.57.att, bf16[512,2048]{1,0:T(8,128)(2,1)} %bitcast.23, ...), custom_call_target="tpu_custom_call" | custom-call | tf_op jit(solution)/shard_map/first_norm_backward/pallas_call | solution.py:1012
  424.7 1.4 fusion.1
  426.1 0.0 copy-start
  426.1 18.6 %widen.1 = (f32[2048,256]{1,0:T(8,128)}, f32[2048,256]{1,0:T(8,128)}, f32[2048,256]{1,0:T(8,128)}, f32[256,2048]{1,0:T(8,128)}, f32[64,2048]{1,0:T(8,128)}, /*in...) custom-call(bf16[8,2,2640,128]{3,2,1,0:T(8,128)(2,1)} %get-tuple-ele, ...), custom_call_target="tpu_custom_call" | custom-call | tf_op jit(solution)/shard_map/widen/pallas_call | solution.py:1056
  444.7 0.0 copy-done
  444.7 0.0 copy-start.1
  444.7 1.3 copy.34
  446.1 1.0 copy-done.1
  447.1 1.3 copy.35
  (2 shorter events, 0.0 us)
Async XLA Ops:
  426.1 18.6 %copy-start = (bf16[8,64,2048]{2,1,0:T(8,128)(2,1)S(1)}, bf16[8,64,2048]{2,1,0:T(8,128)(2,1)}, u32[]{:S(2)}) copy-start(bf16[8,64,2048]{2,1,0:T(8,128)(2,1)} %get-tuple-element.55) | copy-start | bytes 6291460
  444.7 2.3 copy-start.1

commit v3 on v2

--- a/solution.py
+++ b/solution.py
@@ -17,6 +17,7 @@
 SH = 352
 EF = 176
 R1 = 3 * SH + 9 * EF
+RA = 3 * SH
 R2 = 64 + 4 * 256
 VM = 60 * 2**20
 NEG = -1e30
@@ -82,13 +83,6 @@
     pl.semaphore_wait(pltpu.get_barrier_semaphore(), count)
 
 
-def mp_send_parts(parts, landing, ssem, rsem):
-    m = lax.axis_index("mp")
-    for d in range(1, 8):
-        t = mp_at(d)
-        remote(parts.at[t], landing.at[m], ssem.at[d - 1], rsem.at[m], {"mp": t}).start()
-
-
 def mp_send_same(src, landing, ssem, rsem):
     m = lax.axis_index("mp")
     for d in range(1, 8):
@@ -104,6 +98,147 @@
 def mp_wait_send(src, ssem):
     for d in range(1, 8):
         remote(src, src, ssem.at[d - 1], ssem.at[d - 1], {"mp": mp_at(d)}).wait_send()
+
+
+def mp_place():
+    m = lax.axis_index("mp")
+    return lax.div(m, 2), lax.rem(m, 2)
+
+
+def x_peer(dx):
+    x, zh = mp_place()
+    return {"mp": lax.rem(x + dx, 4) * 2 + zh}
+
+
+def zh_peer():
+    x, zh = mp_place()
+    return {"mp": x * 2 + 1 - zh}
+
+
+class MpSum:
+    def __init__(self, parts, refs, ca):
+        self.parts, self.ca = parts, ca
+        self.xa, self.za, self.zb, self.xs, self.xr, self.s, self.r = refs
+        self.x, self.zh = mp_place()
+        self.a, self.b = pl.ds(0, ca), pl.ds(ca, D - ca)
+
+    @staticmethod
+    def scratch(ca):
+        cb, vm = D - ca, pltpu.VMEM
+        return (
+            vm((3, 2, 64, ca), BF), vm((2, 64, ca), BF), vm((4, 64, cb), BF),
+            vm((3, 64, cb), BF), vm((3, 64, cb), BF),
+            pltpu.SemaphoreType.DMA((11,)), pltpu.SemaphoreType.DMA((11,)),
+        )
+
+    def copy(self, n, src, dst, dev):
+        return remote(src, dst, self.s.at[n], self.r.at[n], dev)
+
+    def a_copy(self, dx):
+        far = lax.rem(self.x + dx, 4)
+        src = self.parts.at[pl.ds(far * 2, 2), :, self.a]
+        return self.copy(dx - 1, src, self.xa.at[dx - 1], x_peer(dx))
+
+    def b_copy(self, x):
+        src = self.parts.at[x * 2 + 1 - self.zh, :, self.b]
+        return self.copy(4 + x, src, self.zb.at[x], zh_peer())
+
+    def x_copy(self, dx):
+        return self.copy(7 + dx, self.xs.at[dx - 1], self.xr.at[dx - 1], x_peer(dx))
+
+    def z_copy(self):
+        return self.copy(3, self.za.at[0], self.za.at[1], zh_peer())
+
+    def start_a(self):
+        for dx in range(1, 4):
+            self.a_copy(dx).start()
+
+    def start_b(self):
+        for x in range(4):
+            self.b_copy(x).start()
+
+    def middle(self):
+        for x in range(4):
+            self.b_copy(x).wait_recv()
+        for dx in range(1, 4):
+            far = lax.rem(self.x + dx, 4)
+            val = self.parts[far * 2 + self.zh, :, self.b].astype(F32) + self.zb[far].astype(F32)
+            self.xs[dx - 1] = val.astype(BF)
+            self.x_copy(dx).start()
+        for dx in range(1, 4):
+            self.a_copy(dx).wait_recv()
+        self.za[0] = self.over_x(1 - self.zh).astype(BF)
+        self.z_copy().start()
+
+    def over_x(self, zz):
+        val = self.parts[self.x * 2 + zz, :, self.a].astype(F32)
+        for n in range(3):
+            val = val + self.xa[n, zz].astype(F32)
+        return val
+
+    def finish(self):
+        one = self.over_x(self.zh)
+        two = self.parts[self.x * 2 + self.zh, :, self.b].astype(F32) + self.zb[self.x].astype(F32)
+        for dx in range(1, 4):
+            self.x_copy(dx).wait_recv()
+            two = two + self.xr[dx - 1].astype(F32)
+        self.z_copy().wait_recv()
+        one = one + self.za[1].astype(F32)
+        return jnp.concatenate([one, two], axis=1)
+
+    def drain(self):
+        for dx in range(1, 4):
+            self.a_copy(dx).wait_send()
+            self.x_copy(dx).wait_send()
+        for x in range(4):
+            self.b_copy(x).wait_send()
+        self.z_copy().wait_send()
+
+
+class MpGather:
+    def __init__(self, out, sems, ca):
+        self.out, (self.s, self.r) = out, sems
+        self.x, self.zh = mp_place()
+        self.a, self.b = pl.ds(0, ca), pl.ds(ca, D - ca)
+
+    @staticmethod
+    def sems():
+        return (pltpu.SemaphoreType.DMA((14,)), pltpu.SemaphoreType.DMA((14,)))
+
+    def copy(self, n, x, zh, cols, dev):
+        ref = self.out.at[x * 2 + zh, :, cols]
+        return remote(ref, ref, self.s.at[n], self.r.at[n], dev)
+
+    def start(self):
+        x, zh = self.x, self.zh
+        self.copy(0, x, zh, self.a, zh_peer()).start()
+        for dx in range(1, 4):
+            self.copy(dx, x, zh, self.b, x_peer(dx)).start()
+        self.copy(4, x, zh, self.b, zh_peer()).start()
+        for dx in range(1, 4):
+            self.copy(4 + dx, x, zh, self.a, x_peer(dx)).start()
+
+    def relay(self):
+        x, zh = self.x, self.zh
+        self.copy(0, x, 1 - zh, self.a, zh_peer()).wait_recv()
+        for dx in range(1, 4):
+            self.copy(7 + dx, x, 1 - zh, self.a, x_peer(dx)).start()
+        for dx in (1, 3, 2):
+            back = lax.rem(x + 4 - dx, 4)
+            self.copy(dx, back, zh, self.b, x_peer(dx)).wait_recv()
+            self.copy(10 + dx, back, zh, self.b, zh_peer()).start()
+
+    def finish(self):
+        x, zh = self.x, self.zh
+        self.copy(4, x, 1 - zh, self.b, zh_peer()).wait_recv()
+        for dx in range(1, 4):
+            back = lax.rem(x + 4 - dx, 4)
+            self.copy(4 + dx, back, zh, self.a, x_peer(dx)).wait_recv()
+            self.copy(7 + dx, back, 1 - zh, self.a, x_peer(dx)).wait_recv()
+            self.copy(10 + dx, back, 1 - zh, self.b, zh_peer()).wait_recv()
+        for n in range(14):
+            cols = self.a if n in (0, 5, 6, 7, 8, 9, 10) else self.b
+            self.copy(n, x, zh, cols, zh_peer()).wait_send()
 
 
 class Gather:
@@ -244,6 +379,8 @@
 ANY_SPEC = pl.BlockSpec(memory_space=pl.ANY)
 DMA = pltpu.SemaphoreType.DMA
 MP_SEMS = (DMA((7,)), DMA((8,)))
+CA = 1024
+CO = 1792
 PARTS = pltpu.VMEM((8, 64, D), BF)
 
 
@@ -255,10 +392,14 @@
     return pltpu.roll(x, 64, axis=1)
 
 
+def pick_of(order, k, cr):
+    return jnp.where(order[k * 2 + cr] < order[lax.axis_index("ctx")], 0, 1)
+
+
 def k1_kernel(
-    sel, tokens, wq, wk, wv, wo, cosf, sinf, gain_a, gain_m,
-    moe, mixed, lse, ot, q, kvall, normed, att,
-    tok, w3, wov, st_m, st_l, st_a, parts, land, s_in, g_sems, mp1, mp2,
+    order, tokens, wq, wk, wv, wo, inverse, gain_a, gain_m,
+    moe, mixed, lse, ot, q, kvall, normed, att, cosf, sinf,
+    tok, w3, wov, st_m, st_l, st_a, parts, s_in, g_sems, sum_refs, ag_sems,
 ):
     y, z, core, m = place()
     chip = chip_at(0, 0)
@@ -271,6 +412,13 @@
     for cp in loads:
         cp.start()
     count = greet()
+    pair = order[lax.axis_index("ctx")]
+    sign = jnp.where(lax.broadcasted_iota(jnp.int32, (1, HD), 1) < HD // 2, -1.0, 1.0)
+    for n, first in enumerate((pair, 31 - pair)):
+        pos = (lax.broadcasted_iota(jnp.int32, (256, HD), 0) + first * 256).astype(F32)
+        phase = pos * inverse[...]
+        cosf[pl.ds(n * 256, 256), :] = jnp.cos(phase)
+        sinf[pl.ds(n * 256, 256), :] = jnp.sin(phase) * sign
     loads[0].wait()
 
     def norm_rows(i, carry):
@@ -329,7 +477,7 @@
         st_m[n, h], st_l[n, h], st_a[n, h] = new
 
     def block(k, cr):
-        s = sel[k * 2 + cr]
+        s = pick_of(order, k, cr)
         sts, vs, olds = [], [], []
         for h in range(2):
             cols = pl.ds(h * HD, HD)
@@ -404,24 +552,26 @@
         parts[:, :, cols] = nn(att[...], wov[:, cols]).reshape(8, 64, 256).astype(BF)
         return carry
 
-    lax.fori_loop(0, 8, out_cols, 0)
-    mp_send_parts(parts, land, *mp1)
-    total = tok[pl.ds(pl.multiple_of(m * 64, 64), 64), :].astype(F32) + parts[m].astype(F32)
-    for d in range(1, 8):
-        total = total + land[mp_wait_recv(land, *mp1, d)].astype(F32)
+    mps = MpSum(parts, sum_refs, CA)
+    lax.fori_loop(0, CA // 256, out_cols, 0)
+    mps.start_a()
+    lax.fori_loop(CA // 256, 8, out_cols, 0)
+    mps.start_b()
+    mps.middle()
+    total = tok[pl.ds(pl.multiple_of(m * 64, 64), 64), :].astype(F32) + mps.finish()
     mixed[...] = total
     n = lax.rsqrt(jnp.mean(total * total, axis=-1, keepdims=True) + EPSILON)
     moe[m] = (total * n * gain_m[...]).astype(BF)
-    mp_send_same(moe.at[m], moe, *mp2)
+    mpg = MpGather(moe, ag_sems, CA)
+    mpg.start()
+    mpg.relay()
 
     gather.drain()
-    mp_wait_send(parts.at[0], mp1[0])
-    for d in range(1, 8):
-        mp_wait_recv(moe, *mp2, d)
-    mp_wait_send(moe.at[0], mp2[0])
-
-
-def attention_forward(sel, tokens, wq, wk, wv, wo, cosf, sinf, gain_a, gain_m):
+    mps.drain()
+    mpg.finish()
+
+
+def attention_forward(order, tokens, wq, wk, wv, wo, inverse, gain_a, gain_m):
     return pl.pallas_call(
         k1_kernel,
         name="attend_forward",
@@ -434,9 +584,11 @@
             sds((8, 2, 2, 2, 256, 256), BF),
             sds((512, D), BF),
             sds((512, 256), BF),
+            sds((512, HD), F32),
+            sds((512, HD), F32),
         ),
-        in_specs=[SMEM_SPEC] + [ANY_SPEC] * 5 + [VMEM_SPEC] * 4,
-        out_specs=(VMEM_SPEC,) * 8,
+        in_specs=[SMEM_SPEC] + [ANY_SPEC] * 5 + [VMEM_SPEC] * 3,
+        out_specs=(VMEM_SPEC,) * 10,
         scratch_shapes=[
             pltpu.VMEM((512, D), BF),
             pltpu.VMEM((3, D, 256), BF),
@@ -444,10 +596,10 @@
             pltpu.VMEM((3, 2, 1, 256), F32),
             pltpu.VMEM((3, 2, 1, 256), F32),
             pltpu.VMEM((3, 2, HD, 256), F32),
-            PARTS, PARTS, DMA((5,)), Gather.sems(), MP_SEMS, MP_SEMS,
+            PARTS, DMA((5,)), Gather.sems(), MpSum.scratch(CA), MpGather.sems(),
         ],
         compiler_params=params(1),
-    )(sel, tokens, wq, wk, wv, wo, cosf, sinf, gain_a, gain_m)
+    )(order, tokens, wq, wk, wv, wo, inverse, gain_a, gain_m)
 
 
 def swish_parts(g, u):
@@ -467,8 +619,8 @@
     ids, moe, mixed, gain, w_router, cot, sg, su, sd, eg, eu, ed,
     g_attn, g_mixed, gain_part, wown, moe_part, g_logits,
     wsg, wsu, wsd, weg, weu, wed, cotv, tb, tbt, pr, gt, ut, hs, gsg, gsu,
-    ein, gsl, geo, gated, eo, gein, ge3, ue3, he3, tmp, amat, blk, gate_part, gmi, land, gate_land,
-    s_in, rs_refs, mp1, mp2, mp3,
+    ein, gsl, geo, gated, eo, gein, ge3, ue3, he3, tmp, amat, blk, gate_part, gmi, gate_land,
+    s_in, rs_refs, mp1, sum_refs, ag_sems,
 ):
     y, z, core, m = place()
     loads = [
@@ -589,8 +741,11 @@
         gmi[:, :, cols] = g.reshape(8, 64, 256).astype(BF)
         return carry
 
-    lax.fori_loop(0, 8, back_cols, 0)
-    mp_send_parts(gmi, land, *mp2)
+    mps = MpSum(gmi, sum_refs, CA)
+    lax.fori_loop(0, CA // 256, back_cols, 0)
+    mps.start_a()
+    lax.fori_loop(CA // 256, 8, back_cols, 0)
+    mps.start_b()
 
     amat[pl.ds(0, SH), :] = turned(gsg[...])[0:SH]
     amat[pl.ds(SH, SH), :] = turned(gsu[...])[0:SH]
@@ -647,6 +802,7 @@
     prob = pr[...]
     g_logits[...] = (prob * (gate_probs - jnp.sum(gate_probs * prob, axis=-1, keepdims=True))).astype(BF)
 
+    mps.middle()
     for way, dy in ((0, 1), (1, 3)):
         rs.merge(chip_at(dy, 0))
         rs.merge(chip_at(dy, 1))
@@ -655,9 +811,7 @@
     rs.merge(chip_at(0, 0))
 
     mine = pl.ds(pl.multiple_of(m * 64, 64), 64)
-    total = nn(g_logits[mine, :], w_router[...]) + gmi[m].astype(F32)
-    for d in range(1, 8):
-        total = total + land[mp_wait_recv(land, *mp2, d)].astype(F32)
+    total = nn(g_logits[mine, :], w_router[...]) + mps.finish()
     mx = mixed[...]
     n = lax.rsqrt(jnp.mean(mx * mx, axis=-1, keepdims=True) + EPSILON)
     gain_part[...] = jnp.sum(total * mx * n, axis=0, keepdims=True)
@@ -666,15 +820,15 @@
     gm = gm - mx * (n * n * n) * jnp.mean(gg * mx, axis=-1, keepdims=True)
     g_mixed[...] = gm
     g_attn[m] = gm.astype(BF)
-    mp_send_same(g_attn.at[m], g_attn, *mp3)
+    mpg = MpGather(g_attn, ag_sems, CA)
+    mpg.start()
+    mpg.relay()
 
     rs.own(wown)
     rs.drain()
-    mp_wait_send(gmi.at[0], mp2[0])
+    mps.drain()
     mp_wait_send(gate_part, mp1[0])
-    for d in range(1, 8):
-        mp_wait_recv(g_attn, *mp3, d)
-    mp_wait_send(g_attn.at[0], mp3[0])
+    mpg.finish()
 
 
 def experts(ids, moe, mixed, gain, w_router, cot, sg, su, sd, eg, eu, ed):
@@ -702,18 +856,18 @@
             vm((HD, D), F32), vm((HD, D), BF),
             vm((3, CAP, EF), F32), vm((3, CAP, EF), F32), vm((3, CAP, EF), BF),
             vm((3, HD, 256), F32), vm((3 * SH, 512), BF), vm((9 * EF, HD), BF),
-            vm((1, HD), F32), PARTS, PARTS, vm((8, 1, HD), F32),
-            DMA((7,)), Scatter.scratch(R1, HD), MP_SEMS, MP_SEMS, MP_SEMS,
+            vm((1, HD), F32), PARTS, vm((8, 1, HD), F32),
+            DMA((7,)), Scatter.scratch(R1, HD), MP_SEMS, MpSum.scratch(CA), MpGather.sems(),
         ],
         compiler_params=params(2),
     )(ids, moe, mixed, gain, w_router, cot, sg, su, sd, eg, eu, ed)
 
 
 def k3_kernel(
-    sel, q, kvall, lse, ot, g_attn, wout, moe_part, mixed, wown, cosf, sinf,
-    output, w1, glin,
-    do, delta, dqt, oland, zbuf, fin, dkz, dkv,
-    s_loc, s_z, r_z, s_z2, r_z2, g_sems, rs_refs, mp1, mp2,
+    order, q, kvall, lse, ot, g_attn, wout, moe_part, mixed, wown, cosf, sinf,
+    output, w1, glin, fin_a,
+    do, delta, dqt, zbuf, fin_b, dkz, dkv,
+    s_loc, s_z, r_z, s_z2, r_z2, g_sems, rs_refs, sum_refs, ag_sems,
 ):
     y, z, core, m = place()
     chip = chip_at(0, 0)
@@ -726,7 +880,9 @@
             delta[n, h] = jnp.sum(jnp.transpose(piece.astype(F32)) * ot[n, h], axis=0, keepdims=True)
     dqt[...] = jnp.zeros_like(dqt)
     all_in(count)
-    mp_send_parts(moe_part, oland, *mp1)
+    mps = MpSum(moe_part, sum_refs, CO)
+    mps.start_a()
+    mps.start_b()
     remote(wown.at[1], zbuf, s_z, r_z, peer(0, 1)).start()
     rs = Scatter(rs_refs, 256)
     gather = Gather(w1, g_sems)
@@ -742,7 +898,7 @@
         return list(zip(dk, dv, dq))
 
     def block(k, cr, dst):
-        s = sel[k * 2 + cr]
+        s = pick_of(order, k, cr)
         items = []
         for h in range(2):
             cols = pl.ds(h * HD, HD)
@@ -785,14 +941,18 @@
     rs.far()
     ring_place(1)
     rs.near(0)
+
+    remote(zbuf, zbuf, s_z, r_z, peer(0, 1)).wait_recv()
+    add_rows(fin_a, [wown.at[0, pl.ds(0, RA)], zbuf.at[pl.ds(0, RA)]], 528)
+    add_rows(fin_b, [wown.at[0, pl.ds(RA, R1 - RA)], zbuf.at[pl.ds(RA, R1 - RA)]], 528)
+    gather.start(fin_b)
+    local = pltpu.make_async_copy(fin_b, w1.at[chip, core], s_loc)
+    local.start()
+
     ring_place(3)
     rs.near(1)
-
-    remote(zbuf, zbuf, s_z, r_z, peer(0, 1)).wait_recv()
-    add_rows(fin, [wown.at[0], zbuf], 528)
-    gather.start(fin)
-    local = pltpu.make_async_copy(fin, w1.at[chip, core], s_loc)
-    local.start()
+    gather.hop(0, 1)
+    mps.middle()
 
     both_cores(chip_at(0, 1))
     block(chip, 1 - core, rs.to_sib.at[chip])
@@ -826,13 +986,10 @@
             g = dqt[n, h] if n == 0 else dqt[1, h] + dqt[2, h]
             glin[0, rr, pl.ds(h * HD, HD)] = back(jnp.transpose(g) * (HD**-0.5), rr)
 
-    total = mixed[...] + moe_part[m].astype(F32)
-    for d in range(1, 8):
-        total = total + oland[mp_wait_recv(oland, *mp1, d)].astype(F32)
-    output[m] = total.astype(BF)
-    mp_send_same(output.at[m], output, *mp2)
-
-    gather.hop(0, 1)
+    output[m] = (mixed[...] + mps.finish()).astype(BF)
+    mpg = MpGather(output, ag_sems, CO)
+    mpg.start()
+
     gather.hop(3, 0)
     gather.hop(1, 0)
     rs.own(dkz)
@@ -847,16 +1004,15 @@
             g = dkz[0, kr, cols].astype(F32) + dkv[kr, cols].astype(F32)
             glin[1, rr, cols] = back(g, rr)
             glin[2, rr, cols] = (dkz[0, vr, cols].astype(F32) + dkv[vr, cols].astype(F32)).astype(BF)
+    mpg.relay()
     for dy, t in HOPS[3:]:
         gather.hop(dy, t)
 
     remote(dkv, dkv, s_z2, s_z2, peer(0, 1)).wait_send()
     remote(zbuf, zbuf, s_z, s_z, peer(0, 1)).wait_send()
     rs.drain()
-    mp_wait_send(moe_part.at[0], mp1[0])
-    for d in range(1, 8):
-        mp_wait_recv(output, *mp2, d)
-    mp_wait_send(output.at[0], mp2[0])
+    mps.drain()
+    mpg.finish()
     local.wait()
     gather.wait(chip, 1 - core)
     for dy, t in HOPS:
@@ -864,28 +1020,30 @@
     gather.drain()
 
 
-def attention_backward(sel, q, kvall, lse, ot, g_attn, wout, moe_part, mixed, wown, cosf, sinf):
+def attention_backward(order, q, kvall, lse, ot, g_attn, wout, moe_part, mixed, wown, cosf, sinf):
     vm = pltpu.VMEM
     return pl.pallas_call(
         k3_kernel,
         name="attend_backward",
-        out_shape=(sds((8, 64, D), BF), sds((8, 2, R1, HD), BF), sds((3, 512, 256), BF)),
+        out_shape=(
+            sds((8, 64, D), BF), sds((8, 2, R1 - RA, HD), BF), sds((3, 512, 256), BF), sds((RA, HD), BF),
+        ),
         in_specs=[SMEM_SPEC] + [VMEM_SPEC] * 11,
-        out_specs=(VMEM_SPEC, ANY_SPEC, VMEM_SPEC),
+        out_specs=(VMEM_SPEC, ANY_SPEC, VMEM_SPEC, VMEM_SPEC),
         scratch_shapes=[
             vm((2, 2, 256, HD), BF), vm((2, 2, 1, 256), F32), vm((3, 2, HD, 256), F32),
-            PARTS, vm((R1, HD), BF), vm((R1, HD), BF), vm((2, 1024, 256), BF), vm((1024, 256), BF),
-            DMA, DMA, DMA, DMA, DMA, Gather.sems(), Scatter.scratch(1024, 256), MP_SEMS, MP_SEMS,
+            vm((R1, HD), BF), vm((R1 - RA, HD), BF), vm((2, 1024, 256), BF), vm((1024, 256), BF),
+            DMA, DMA, DMA, DMA, DMA, Gather.sems(), Scatter.scratch(1024, 256), MpSum.scratch(CO), MpGather.sems(),
         ],
         compiler_params=params(3),
-    )(sel, q, kvall, lse, ot, g_attn, wout, moe_part, mixed, wown, cosf, sinf)
+    )(order, q, kvall, lse, ot, g_attn, wout, moe_part, mixed, wown, cosf, sinf)
 
 
 def k4_kernel(
-    glin, att, g_attn, g_logits, moe, normed, g_mixed, gain, gain_moe_part, tokens, wq, wk, wv,
-    g_tokens, w2out, gains,
-    tok, w3, amat, gni, land, zbuf, fin, wown, gmine, gland, gsteps, gfar,
-    s_in, s_loc, s_z, r_z, s_gx, r_gx, s_gy, r_gy, g_sems, rs_refs, mp1, mp2, mp3,
+    glin, att, g_attn, g_logits, moe, normed, g_mixed, gain, gain_moe_part, fin_a, tokens, wq, wk, wv,
+    g_tokens, w2out, gains, w1a,
+    tok, w3, amat, gni, zbuf, fin, wown, gmine, gland, gsteps, gfar,
+    s_in, s_loc, s_loc2, s_z, r_z, s_gx, r_gx, s_gy, r_gy, g_sems, g_sems2, rs_refs, sum_refs, ag_sems, mp3,
 ):
     y, z, core, m = place()
     chip = chip_at(0, 0)
@@ -906,9 +1064,16 @@
         gni[:, :, cols] = g.reshape(8, 64, 256).astype(BF)
         return carry
 
-    lax.fori_loop(0, 8, back_cols, 0)
+    mps = MpSum(gni, sum_refs, CA)
+    lax.fori_loop(0, CA // 256, back_cols, 0)
     all_in(count)
-    mp_send_parts(gni, land, *mp1)
+    mps.start_a()
+    lax.fori_loop(CA // 256, 8, back_cols, 0)
+    mps.start_b()
+    first = Gather(w1a, g_sems2)
+    first.start(fin_a)
+    local2 = pltpu.make_async_copy(fin_a, w1a.at[chip, core], s_loc2)
+    local2.start()
 
     amat[pl.ds(0, 64), :] = turned(g_logits[...])
     for i in range(3):
@@ -939,41 +1104,43 @@
         return carry
 
     lax.fori_loop(0, 8, pieces, 0)
+    first.hop(0, 1)
     for way, dy in ((0, 1), (1, 3)):
         rs.merge(chip_at(dy, 0))
         rs.merge(chip_at(dy, 1))
         rs.near(way)
+        first.hop(3 if way == 0 else 1, 0)
+        if way == 0:
+            mps.middle()
     rs.merge(chip_at(0, 1))
     rs.merge(chip_at(0, 0))
 
-    total = gni[m].astype(F32)
-    for d in range(1, 8):
-        total = total + land[mp_wait_recv(land, *mp1, d)].astype(F32)
+    total = mps.finish()
     src = tok[...].astype(F32)
     n = lax.rsqrt(jnp.mean(src * src, axis=-1, keepdims=True) + EPSILON)
     gg = total * gain[...]
     gs = n * gg - src * (n * n * n) * jnp.mean(gg * src, axis=-1, keepdims=True)
     g_tokens[m] = (g_mixed[...] + gs).astype(BF)
-    mp_send_same(g_tokens.at[m], g_tokens, *mp2)
     gmine[pl.ds(0, 1), :] = gain_moe_part[...]
     gmine[pl.ds(1, 1), :] = jnp.sum(total * src * n, axis=0, keepdims=True)
     mp_send_same(gmine, gland, *mp3)
+    mpg = MpGather(g_tokens, ag_sems, CA)
+    mpg.start()
+    first.hop(3, 1)
+    first.hop(1, 1)
+    mpg.relay()
 
     rs.own(wown)
     remote(wown.at[1], zbuf, s_z, r_z, peer(0, 1)).start()
+
+    def gain_step(i, dev):
+        return remote(gsteps.at[2 * i], gsteps.at[2 * i + 1], s_gx.at[i], r_gx.at[i], dev)
 
     gsum = gmine[...]
     for d in range(1, 8):
         gsum = gsum + gland[mp_wait_recv(gland, *mp3, d)]
-    for i, dev in enumerate((sibling(), peer(0, 1))):
-        gsteps[2 * i] = gsum
-        cp = remote(gsteps.at[2 * i], gsteps.at[2 * i + 1], s_gx.at[i], r_gx.at[i], dev)
-        cp.start()
-        cp.wait_recv()
-        gsum = gsum + gsteps[2 * i + 1]
-    gfar[y] = gsum
-    for d in range(1, 4):
-        remote(gfar.at[y], gfar.at[y], s_gy.at[d - 1], r_gy.at[y], peer(d, 0)).start()
+    gsteps[0] = gsum
+    gain_step(0, sibling()).start()
 
     remote(zbuf, zbuf, s_z, r_z, peer(0, 1)).wait_recv()
     add_rows(fin, [wown.at[0], zbuf], 544)
@@ -982,13 +1149,22 @@
     local = pltpu.make_async_copy(fin, w2out.at[chip, core], s_loc)
     local.start()
 
+    gain_step(0, sibling()).wait_recv()
+    gsteps[2] = gsteps[0] + gsteps[1]
+    gain_step(1, peer(0, 1)).start()
+    first.hop(2, 0)
+    first.hop(2, 1)
+    gain_step(1, peer(0, 1)).wait_recv()
+    gfar[y] = gsteps[2] + gsteps[3]
+    for d in range(1, 4):
+        remote(gfar.at[y], gfar.at[y], s_gy.at[d - 1], r_gy.at[y], peer(d, 0)).start()
+    for dy, t in HOPS:
+        gather.hop(dy, t)
     for d in range(1, 4):
         yy = lax.rem(y + d, 4)
         remote(gfar.at[yy], gfar.at[yy], s_gy.at[0], r_gy.at[yy], peer(d, 0)).wait_recv()
     gains[...] = gfar[0] + gfar[1] + gfar[2] + gfar[3]
 
-    for dy, t in HOPS:
-        gather.hop(dy, t)
     for i, dev in enumerate((sibling(), peer(0, 1))):
         remote(gsteps.at[0], gsteps.at[0], s_gx.at[i], s_gx.at[i], dev).wait_send()
     for d in range(1, 4):
@@ -996,15 +1172,15 @@
     remote(zbuf, zbuf, s_z, s_z, peer(0, 1)).wait_send()
     rs.drain()
     mp_wait_send(gmine, mp3[0])
-    mp_wait_send(gni.at[0], mp1[0])
-    for d in range(1, 8):
-        mp_wait_recv(g_tokens, *mp2, d)
-    mp_wait_send(g_tokens.at[0], mp2[0])
+    mps.drain()
+    mpg.finish()
     local.wait()
-    gather.wait(chip, 1 - core)
-    for dy, t in HOPS:
-        gather.other_core(dy, t)
-    gather.drain()
+    local2.wait()
+    for g in (first, gather):
+        g.wait(chip, 1 - core)
+        for dy, t in HOPS:
+            g.other_core(dy, t)
+        g.drain()
 
 
 def first_norm_backward(*args):
@@ -1012,20 +1188,25 @@
     return pl.pallas_call(
         k4_kernel,
         name="first_norm_backward",
-        out_shape=(sds((8, 64, D), BF), sds((8, 2, R2, HD), BF), sds((2, D), F32)),
-        in_specs=[VMEM_SPEC] * 9 + [ANY_SPEC] * 4,
-        out_specs=(VMEM_SPEC, ANY_SPEC, VMEM_SPEC),
+        out_shape=(
+            sds((8, 64, D), BF), sds((8, 2, R2, HD), BF), sds((2, D), F32), sds((8, 2, RA, HD), BF),
+        ),
+        in_specs=[VMEM_SPEC] * 10 + [ANY_SPEC] * 4,
+        out_specs=(VMEM_SPEC, ANY_SPEC, VMEM_SPEC, ANY_SPEC),
         scratch_shapes=[
-            vm((64, D), BF), vm((3, D, 256), BF), vm((R2, 512), BF), PARTS, PARTS, vm((R2, HD), BF), vm((R2, HD), BF),
+            vm((64, D), BF), vm((3, D, 256), BF), vm((R2, 512), BF), PARTS, vm((R2, HD), BF), vm((R2, HD), BF),
             vm((2, R2, HD), BF), vm((2, D), F32), vm((8, 2, D), F32), vm((4, 2, D), F32), vm((4, 2, D), F32),
-            DMA((4,)), DMA, DMA, DMA, DMA((2,)), DMA((2,)), DMA((3,)), DMA((4,)),
-            Gather.sems(), Scatter.scratch(R2, HD), MP_SEMS, MP_SEMS, MP_SEMS,
+            DMA((4,)), DMA, DMA, DMA, DMA, DMA((2,)), DMA((2,)), DMA((3,)), DMA((4,)),
+            Gather.sems(), Gather.sems(), Scatter.scratch(R2, HD), MpSum.scratch(CA), MpGather.sems(), MP_SEMS,
         ],
         compiler_params=params(4),
     )(*args)
 
 
-def widen_kernel(w1, w2, gq, gk, gv, go, gr, sg, su, sd, eg, eu, ed):
+def widen_kernel(
+    wa, wb, w2, out_in, tok_in, gains,
+    gq, gk, gv, go, gr, sg, su, sd, eg, eu, ed, out, tok, gain_a, gain_m,
+):
     def flip(src, off):
         return jnp.transpose(src[0, 0, pl.ds(off, 256), :].astype(F32))
 
@@ -1034,16 +1215,18 @@
     gk[...] = flip(w2, 320)
     gv[...] = flip(w2, 576)
     go[...] = w2[0, 0, pl.ds(832, 256), :].astype(F32)
-    sg[...] = w1[0, 0, pl.ds(0, SH), :].astype(F32)
-    su[...] = w1[0, 0, pl.ds(SH, SH), :].astype(F32)
-    sd[...] = w1[0, 0, pl.ds(2 * SH, SH), :].astype(F32)
+    for k, ref in enumerate((sg, su, sd)):
+        ref[...] = wa[0, 0, pl.ds(k * SH, SH), :].astype(F32)
     for k in range(3):
-        eg[k] = w1[0, 0, pl.ds(3 * SH + EF * k, EF), :].astype(F32)
-        eu[k] = w1[0, 0, pl.ds(3 * SH + EF * (3 + k), EF), :].astype(F32)
-        ed[k] = w1[0, 0, pl.ds(3 * SH + EF * (6 + k), EF), :].astype(F32)
-
-
-def widen(w1, w2):
+        for j, ref in enumerate((eg, eu, ed)):
+            ref[k] = wb[0, 0, pl.ds(EF * (3 * j + k), EF), :].astype(F32)
+    out[...] = out_in[...]
+    tok[...] = tok_in[...]
+    gain_m[...] = gains[pl.ds(0, 1), :]
+    gain_a[...] = gains[pl.ds(1, 1), :]
+
+
+def widen(wa, wb, w2, out_in, tok_in, gains):
     def rows(width):
         return sds((D, width), F32), pl.BlockSpec((HD, width), lambda i: (i, 0))
 
@@ -1051,20 +1234,22 @@
         return sds((height, D), F32), pl.BlockSpec((height, HD), lambda i: (0, i))
 
     three = sds((3, EF, D), F32), pl.BlockSpec((3, EF, HD), lambda i: (0, 0, i))
+    whole = pl.BlockSpec((32, D), lambda i: (i, 0))
+    gain = sds((1, D), F32), pl.BlockSpec((1, HD), lambda i: (0, i))
     outs = [rows(256), rows(256), rows(256), cols(256), cols(64), cols(SH), cols(SH), cols(SH)]
-    outs += [three, three, three]
+    outs += [three, three, three, (sds((512, D), BF), whole), (sds((512, D), BF), whole), gain, gain]
     return pl.pallas_call(
         widen_kernel,
         name="widen",
         grid=(16,),
         out_shape=[o[0] for o in outs],
         in_specs=[
-            pl.BlockSpec((1, 1, R1, HD), lambda i: (i // 2, i % 2, 0, 0)),
-            pl.BlockSpec((1, 1, R2, HD), lambda i: (i // 2, i % 2, 0, 0)),
-        ],
+            pl.BlockSpec((1, 1, w.shape[2], HD), lambda i: (i // 2, i % 2, 0, 0)) for w in (wa, wb, w2)
+        ]
+        + [whole, whole, pl.BlockSpec((2, HD), lambda i: (0, i))],
         out_specs=[o[1] for o in outs],
         compiler_params=pltpu.CompilerParams(vmem_limit_bytes=VM),
-    )(w1, w2)
+    )(wa, wb, w2, out_in, tok_in, gains)
 
 
 def on_device(
@@ -1072,19 +1257,10 @@
     shared_gate, shared_up, shared_down, expert_gate, expert_up, expert_down, expert_ids, pair_order,
 ):
     rows = tokens.shape[0]
-    member = lax.axis_index("ctx")
-    pair = lax.dynamic_index_in_dim(pair_order, member, keepdims=False)
-    within = jnp.arange(rows, dtype=jnp.int32)
-    pos = jnp.where(within < 256, pair * 256 + within, (31 - pair) * 256 + within - 256)
     inverse = ROPE_BASE ** (-2.0 * jnp.arange(HD // 2, dtype=F32) / HD)
-    phase = pos.astype(F32)[:, None] * jnp.concatenate([inverse, inverse])[None, :]
-    sign = jnp.where(jnp.arange(HD) < HD // 2, -1.0, 1.0).astype(F32)
-    cosf = jnp.cos(phase)
-    sinf = jnp.sin(phase) * sign[None, :]
-    sel = jnp.where(pair_order < pair, 0, 1).astype(jnp.int32)
-
-    moe, mixed, lse, ot, q, kvall, normed, att = attention_forward(
-        sel, tokens, w_query, w_key, w_value, w_out, cosf, sinf, gain_attn[None], gain_moe[None]
+    inverse = jnp.concatenate([inverse, inverse])[None]
+    moe, mixed, lse, ot, q, kvall, normed, att, cosf, sinf = attention_forward(
+        pair_order, tokens, w_query, w_key, w_value, w_out, inverse, gain_attn[None], gain_moe[None]
     )
     moe = moe.reshape(rows, D)
     g_attn, g_mixed, gain_moe_part, wown, moe_part, g_logits = experts(
@@ -1092,17 +1268,19 @@
         expert_gate.transpose(0, 2, 1), expert_up.transpose(0, 2, 1), expert_down,
     )
     g_attn = g_attn.reshape(rows, D)
-    output, w1, glin = attention_backward(
-        sel, q, kvall, lse, ot, g_attn, w_out, moe_part, mixed, wown, cosf, sinf
+    output, wb, glin, fin_a = attention_backward(
+        pair_order, q, kvall, lse, ot, g_attn, w_out, moe_part, mixed, wown, cosf, sinf
     )
-    g_tokens, w2, gains = first_norm_backward(
-        glin, att, g_attn, g_logits, moe, normed, g_mixed, gain_attn[None], gain_moe_part,
+    g_tokens, w2, gains, wa = first_norm_backward(
+        glin, att, g_attn, g_logits, moe, normed, g_mixed, gain_attn[None], gain_moe_part, fin_a,
         tokens, w_query, w_key, w_value,
     )
-    gq, gk, gv, go, gr, sg, su, sd, eg, eu, ed = widen(w1, w2)
+    gq, gk, gv, go, gr, sg, su, sd, eg, eu, ed, output, g_tokens, gain_a, gain_m = widen(
+        wa, wb, w2, output.reshape(rows, D), g_tokens.reshape(rows, D), gains
+    )
     return (
-        output.reshape(rows, D), g_tokens.reshape(rows, D), gains[1],
-        gq, gk, gv, go, gains[0], gr.T, sg.T, su.T, sd, eg.transpose(0, 2, 1), eu.transpose(0, 2, 1), ed,
+        output, g_tokens, gain_a.reshape(D), gq, gk, gv, go, gain_m.reshape(D), gr.T,
+        sg.T, su.T, sd, eg.transpose(0, 2, 1), eu.transpose(0, 2, 1), ed,
     )
 
 

time: 449 us -> 378 us (0.84)
  Pallas kernels: 436 us -> 376 us
  local copies, waits for them, and re-layouts: 6.31 us -> 0 us
    pallas_call x1, Pallas kernels: 120 us -> 90.6 us  [attention_backward(): pl.pallas_call(k3_kernel, name='attend_backward', out_shape=(sds((8, 64,...]
    pallas_call x1, Pallas kernels: 119 us -> 101 us  [attention_forward(): pl.pallas_call(k1_kernel, name='attend_forward', out_shape=(sds((8, 64, D...]
    pallas_call x1, Pallas kernels: 100 us -> 86.9 us  [first_norm_backward(): pl.pallas_call(k4_kernel, name='first_norm_backward', out_shape=(sds((8,...]
where the time goes in v3:
time: 378 us; the launch traced here: 377 us
  Pallas kernels  376 us (99%)
    pallas_call x1, Pallas kernels, attention_forward(): pl.pallas_call(k1_kernel, name='attend_forward', out_shape=(sds((8, 64, D...  101 us
    pallas_call x1, Pallas kernels, attention_backward(): pl.pallas_call(k3_kernel, name='attend_backward', out_shape=(sds((8, 64,...  90.6 us
    pallas_call x1, Pallas kernels, first_norm_backward(): pl.pallas_call(k4_kernel, name='first_norm_backward', out_shape=(sds((8,...  86.9 us
    pallas_call x1, Pallas kernels, experts(): pl.pallas_call(k2_kernel, name='experts', out_shape=(sds((8, 64, D), BF),...  76.4 us
    pallas_call x1, Pallas kernels, widen(): pl.pallas_call(widen_kernel, name='widen', grid=(16,), out_shape=[o[0] fo...  20.9 us

profile of v3, /device:TPU:1, one launch (start us, length us, event | category | flops | bytes accessed | tf_op | source)
XLA Modules:
  0.0 377.1 jit_solution(15885264371853893918)
XLA Ops:
  0.7 0.6 maximum_bitcast_fusion.inverse
  1.2 100.8 %attend_forward.1 = (bf16[8,64,2048]{2,1,0:T(8,128)(2,1)}, f32[64,2048]{1,0:T(8,128)}, f32[2,2,1,256]{3,2,1,0:T(1,128)}, f32[2,2,128,256]{3,2,1,0:T(8,128)}, bf1...) custom-call(s32[16]{0:T(128)} %order.3, ...), custom_call_target="tpu_custom_call" | custom-call | tf_op jit(solution)/shard_map/attend_forward/pallas_call | solution.py:575
  102.1 76.4 %experts.1 = (bf16[8,64,2048]{2,1,0:T(8,128)(2,1)}, f32[64,2048]{1,0:T(8,128)}, f32[1,2048]{1,0:T(1,128)}, bf16[2,2640,128]{2,1,0:T(8,128)(2,1)}, bf16[8,64,2048]{2,1,0:T(8,128)(2,1)}, /*index=5*/bf16[512,64]{1,0:T(8,128)(2,1)}) custom-call(s32[6,512]{1,0:T(8,128)} %bitcast.36, bf16[512,2048]{1,0:T(8,128)(2,1)} %bitcast.21, ...), custom_call_target="tpu_custom_call" | custom-call | tf_op jit(solution)/shard_map/experts/pallas_call | solution.py:836
  178.5 90.6 %attend_backward.1 = (bf16[8,64,2048]{2,1,0:T(8,128)(2,1)}, bf16[8,2,1584,128]{3,2,1,0:T(8,128)(2,1)}, bf16[3,512,256]{2,1,0:T(8,128)(2,1)}, bf16[1056,128]{1,0:T(8,128)(2,1)}) custom-call(s32[16]{0:T(128)} %order.3, bf16[2,256,256]{2,1,0:T(8,128)(2,1)} %get-tuple-element.54.q, bf16[8,2,2,2,256,256]{5,4,3,2,1,0:T(8,128)(2,1)} %get-tuple-element.55.kvall, ...), custom_call_target="tpu_custom_call" | custom-call | tf_op jit(solution)/shard_map/attend_backward/pallas_call | solution.py:1025
  269.0 86.9 %first_norm_backward.1 = (bf16[8,64,2048]{2,1,0:T(8,128)(2,1)}, bf16[8,2,1088,128]{3,2,1,0:T(8,128)(2,1)}, f32[2,2048]{1,0:T(2,128)}, bf16[8,2,1056,128]{3,2,1,0:T(8,128)(2,1)}) custom-call(bf16[3,512,256]{2,1,0:T(8,128)(2,1)} %get-tuple-element.65.glin, bf16[512,256]{1,0:T(8,128)(2,1)} %get-tuple-element.66.att, bf16[512,2048]{1,0:T(8,128)(2,1)} %bitcast.24, ...), custom_call_target="tpu_custom_call" | custom-call | tf_op jit(solution)/shard_map/first_norm_backward/pallas_call | solution.py:1188
  356.0 20.9 %widen.1 = (f32[2048,256]{1,0:T(8,128)}, f32[2048,256]{1,0:T(8,128)}, f32[2048,256]{1,0:T(8,128)}, f32[256,2048]{1,0:T(8,128)}, f32[64,2048]{1,0:T(8,128)}, /*in...) custom-call(bf16[8,2,1056,128]{3,2,1,0:T(8,128)(2,1)} %get-tuple-ele, ...), custom_call_target="tpu_custom_call" | custom-call | tf_op jit(solution)/shard_map/widen/pallas_call | solution.py:1241
  (1 shorter events, 0.0 us)
